TPU v7x, 128 devices: a whole 4x4x4 slice. The times are simulated.
128 devices in a mesh: bucket: 8 (over z, y_lo), dom: 16 (over y_hi, x, core).
Axes of the slice: x: 4, y: 4 (y_hi: 2, y_lo: 2; y = y_hi * 2 + y_lo), z: 4, core: 2. Of those that a mesh axis runs over, the one named last changes fastest.
Arguments:
- entity_table: float32 [16, 512, 400], P('bucket', 'dom'), may hold values from -3 to 3
- adagrad_state: float32 [16, 512], P('bucket', 'dom'), may hold values from 0.1 to 10
- relations: float32 [7424, 400], replicated, may hold values from -3 to 3
- roster: int32 [4, 8, 2], replicated, may hold values from 0 to 15, as said below
- edge_triples: int32 [128, 128, 4, 8, 3], P(('bucket', 'dom')), may hold values from 0 to 8191, as said below
- counts: int32 [128, 128, 4], P(('bucket', 'dom')), may hold values from 0 to 8, as said below
- negatives: int32 [4, 8, 16, 16, 512], P(None, 'bucket', 'dom'), may hold values from 0 to 511
Outputs:
- updated_table: float32 [16, 512, 400], P('bucket', 'dom')
- updated_state: float32 [16, 512], P('bucket', 'dom')
Inputs may be any that keep to these rules, and one draw needn't show every extreme that they name: In each step every partition 0 to 15 appears exactly once in roster[s]. `edge_triples`: for receiving device w * 16 + j and step s, every head lies in partition roster[s, w, 0] and every tail in partition roster[s, w, 1]; relation ids lie in 0 to 7423, entity ids in 0 to 8191. `counts`: in every step some receiving device gets 8 live slots from every sending device.
All inputs are finite; a program needn't handle non-finite values.
Results may differ from a plain program's by a relative error of at most 0.0003.
Values sent between devices are 32-bit elements; how exact they have to be, the bound alone decides.
No kernel may reach another device: no remote copies, remote signals or barrier semaphores. Data moves between devices by JAX's collectives and lax.ppermute only.
A program may use at most 128 MiB of HBM per device.

v0:
```python
import functools

import jax
import jax.numpy as jnp
from jax import lax
from jax.experimental import pallas as pl
from jax.experimental.pallas import tpu as pltpu
from jax.sharding import PartitionSpec as P

cubic_weight = 0.1
learn_rate = 0.05
epsilon = 1e-06

HALF = 200
LANES = 128
SHARD = 32
PROWS = 512
SLOTS = 1024
MIB = 1024 * 1024

VMEM = pl.BlockSpec(memory_space=pltpu.VMEM)
SMEM = pl.BlockSpec(memory_space=pltpu.SMEM)


def dom_perms():
    def move(fn):
        return [(j, fn(j)) for j in range(16)]

    def shift(j, d):
        return (j // 8) * 8 + (((j // 2) % 4 + d) % 4) * 2 + j % 2

    return dict(
        axis="dom",
        plus=move(lambda j: shift(j, 1)),
        minus=move(lambda j: shift(j, 3)),
        far=move(lambda j: shift(j, 2)),
        flip=move(lambda j: j ^ 8),
        core=move(lambda j: j ^ 1),
    )


def bucket_perms():
    def move(fn):
        return [(w, fn(w)) for w in range(8)]

    return dict(
        axis="bucket",
        plus=move(lambda w: (w + 2) % 8),
        minus=move(lambda w: (w + 6) % 8),
        far=move(lambda w: (w + 4) % 8),
        flip=move(lambda w: w ^ 1),
    )


def tied(value, *extra):
    out = lax.optimization_barrier((value,) + extra)
    return out[0], out[1:]


def spread(block, perms, early=None, late=None):
    def go(v, name):
        return lax.ppermute(v, perms["axis"], perms[name])

    y = go(block, "flip")
    if early is not None:
        y, (early,) = tied(y, early)
    both = jnp.concatenate([block, y], axis=0)
    r, l, f = go(both, "plus"), go(both, "minus"), go(both, "far")
    if late is not None:
        f, (late,) = tied(f, late)
    return [both, r, l, f], early, late


def dom_gather(block, early=None):
    perms = dom_perms()
    mine, early, _ = spread(block, perms, early)
    return early, mine + [lax.ppermute(v, "dom", perms["core"]) for v in mine]


def dom_reduce(own, other, early=None, late=None):
    perms = dom_perms()

    def go(v, name):
        return lax.ppermute(v, "dom", perms[name])

    swapped = [go(v, "core") for v in other]
    to_plus, to_minus = own[0] + swapped[0], own[1] + swapped[1]
    plus, minus = go(to_plus, "plus"), go(to_minus, "minus")
    on_plus = own[2][0] + swapped[2][0] + plus[0]
    on_minus = own[2][1] + swapped[2][1] + minus[0]
    if early is not None:
        on_plus, (on_minus, early) = tied(on_plus, on_minus, early)
    u4, u3 = go(on_plus, "plus"), go(on_minus, "minus")
    flipped = (own[2][2] + swapped[2][2]) + (plus[1] + u3)
    if late is not None:
        flipped, (late,) = tied(flipped, late)
    return (own[2], swapped[2], minus, u4, go(flipped, "flip")), early, late


OUT_PLACE = {6: (0, 0), 5: (0, 1), 7: (1, 0), 2: (1, 1), 4: (2, 0), 3: (2, 1), 1: (2, 2), 0: (2, 3)}


def ring_place(ring):
    return jnp.where(ring == 0, 0, jnp.where(ring == 3, 1, jnp.where(ring == 1, 2, 3)))


def place_dom(rows, me):
    owner = rows >> 5
    ring = ((owner >> 1) - (me >> 1)) & 3
    flip = ((owner >> 3) ^ (me >> 3)) & 1
    core = (owner ^ me) & 1
    return ((core << 3) + (ring_place(ring) << 1) + flip) * SHARD + (rows & (SHARD - 1))


def place_bucket(source, me):
    return (ring_place(((source >> 1) - (me >> 1)) & 3) << 1) + ((source ^ me) & 1)


def lane_index(shape):
    return lax.broadcasted_iota(jnp.int32, shape, 1)


def views(arrays, rows):
    return [(ref, at) for ref in arrays for at in range(0, ref.shape[0], rows)]


def read(ref, at, rows):
    return ref[at:at + rows]


def select_kernel(exchange, steps, roster, *refs):
    blocks, (x_ref, st_ref) = views(refs[:-2], HALF + 8), refs[-2:]
    me = lax.axis_index("bucket")
    lane = lane_index((HALF + 8, LANES))
    picked = []
    for q in range(2):
        wanted = 2 * me + q if exchange == steps else roster[exchange, 2 * me + q]
        at = jnp.int32(0)
        for i in range(16):
            label = i if exchange == 0 else roster[exchange - 1, i]
            at = jnp.where(wanted == label, jnp.int32(i), at)
        place, half = place_bucket(at >> 1, me), at & 1
        got = read(*blocks[0], HALF + 8)
        for p in range(1, 8):
            got = jnp.where(place == p, read(*blocks[p], HALF + 8), got)
        picked.append(jnp.where(half == q, got, pltpu.roll(got, 32 if q else 96, 1)))
    out = jnp.where((lane // SHARD) % 2 == 0, picked[0], picked[1])
    x_ref[...] = out[:HALF]
    st_ref[...] = out[HALF:]


def select_blocks(blocks, roster, exchange):
    return pl.pallas_call(
        functools.partial(select_kernel, exchange, roster.shape[0]),
        out_shape=(
            jax.ShapeDtypeStruct((HALF, LANES), jnp.float32),
            jax.ShapeDtypeStruct((8, LANES), jnp.float32),
        ),
        in_specs=[SMEM] + [VMEM] * len(blocks),
        out_specs=(VMEM, VMEM),
        compiler_params=pltpu.CompilerParams(vmem_limit_bytes=4 * MIB),
        cost_estimate=pl.CostEstimate(flops=200000, bytes_accessed=500000, transcendentals=0),
    )(roster, *blocks)


def adagrad_kernel(own, swapped, minus, ring, flipped, x_ref, st_ref, out_ref):
    grad = (own[3] + swapped[3]) + ((minus[1] + ring[...]) + flipped[...])
    total = jnp.sum(grad * grad, axis=0, keepdims=True)
    total = jnp.broadcast_to(total, (8, LANES))
    total = total + pltpu.roll(total, 64, 1)
    state = st_ref[...] + total / (2.0 * HALF)
    scale = learn_rate / jnp.sqrt(state + epsilon)
    out_ref[:HALF] = x_ref[...] - grad * scale[0:1]
    out_ref[HALF:] = state


def adagrad(parts, x, st):
    return pl.pallas_call(
        adagrad_kernel,
        out_shape=jax.ShapeDtypeStruct((HALF + 8, LANES), jnp.float32),
        in_specs=[VMEM] * 7,
        out_specs=VMEM,
        compiler_params=pltpu.CompilerParams(vmem_limit_bytes=4 * MIB),
        cost_estimate=pl.CostEstimate(flops=200000, bytes_accessed=700000, transcendentals=0),
    )(*parts, x, st)


def split(v):
    high = v.astype(jnp.bfloat16)
    return high, (v - high.astype(jnp.float32)).astype(jnp.bfloat16)


def nn(a, b):
    return lax.dot_general(a, b, (((1,), (0,)), ((), ())), preferred_element_type=jnp.float32)


def nt(a, b):
    return lax.dot_general(a, b, (((1,), (1,)), ((), ())), preferred_element_type=jnp.float32)


def tn(a, b):
    return lax.dot_general(a, b, (((0,), (0,)), ((), ())), preferred_element_type=jnp.float32)


def three(fn, a, b):
    return fn(a[0], b[0]) + (fn(a[0], b[1]) + fn(a[1], b[0]))


def exchange_lanes(tiles):
    lane = lane_index((HALF, LANES))
    low, even = lane < 2 * SHARD, (lane // SHARD) % 2 == 0
    a, b, c, d = tiles
    a, c = jnp.where(low, a, pltpu.roll(c, 64, 1)), jnp.where(low, pltpu.roll(a, 64, 1), c)
    b, d = jnp.where(low, b, pltpu.roll(d, 64, 1)), jnp.where(low, pltpu.roll(b, 64, 1), d)
    a, b = jnp.where(even, a, pltpu.roll(b, 32, 1)), jnp.where(even, pltpu.roll(a, 96, 1), b)
    c, d = jnp.where(even, c, pltpu.roll(d, 32, 1)), jnp.where(even, pltpu.roll(c, 96, 1), d)
    return a, b, c, d


def step_kernel(step, steps, roster, arrived, drawn, *refs):
    arrays, rel, outs, scratch = refs[:-15], refs[-15], refs[-14:-8], refs[-8:]
    blocks = views(arrays, HALF)
    src, dst, sh, sl, dh, dl, th, tl = scratch
    me = lax.axis_index("bucket")
    dom = lax.axis_index("dom")
    base = step * 24

    def row(v):
        return jnp.concatenate([v[i:i + 1] for i in range(8)], axis=1)

    heads = row(place_dom(arrived[base:base + 8] - roster[step, 2 * me] * PROWS, dom))
    tails = row(place_dom(arrived[base + 16:base + 24] - roster[step, 2 * me + 1] * PROWS, dom))
    slot = lax.broadcasted_iota(jnp.int32, (8, LANES), 0)
    live_slot = row(jnp.where(slot < arrived[24 * steps + step:24 * steps + step + 1], 1.0, 0.0))

    quarters = ((src, 0), (dst, 0), (src, HALF), (dst, HALF))
    for t in range(4):
        tiles = exchange_lanes([read(*blocks[4 * t + g], HALF) for g in range(4)])
        for (to, at), tile in zip(quarters, tiles):
            to[at:at + HALF, t * LANES:(t + 1) * LANES] = tile

    sh[...], sl[...] = split(src[...])
    dh[...], dl[...] = split(dst[...])
    th[...], tl[...] = split(dst[...].T)
    count = split(drawn[...])
    mine = lax.broadcasted_iota(jnp.int32, (16, LANES), 0) == lax.broadcasted_iota(jnp.int32, (16, LANES), 1) // 8
    mine = jnp.where(mine, 1.0, 0.0).astype(jnp.bfloat16)
    weight = tn(count[0], mine) + tn(count[1], mine)

    column = lax.broadcasted_iota(jnp.int32, (PROWS, SLOTS), 0)
    head_hot = jnp.where(column == heads, 1.0, 0.0).astype(jnp.bfloat16)
    tail_hot = jnp.where(column == tails, 1.0, 0.0)
    head = nn(sh[...], head_hot) + nn(sl[...], head_hot)
    turn = rel[...].T
    h_re, h_im, r_re, r_im = head[:HALF], head[HALF:], turn[:HALF], turn[HALF:]
    query = split(jnp.concatenate([h_re * r_re - h_im * r_im, h_re * r_im + h_im * r_re], axis=0))
    scores = three(nn, (th[...], tl[...]), query)
    amount = jnp.concatenate([weight] * 8, axis=1) + tail_hot
    scores = jnp.where(amount > 0, scores, -1e30)
    top = jnp.max(scores, axis=0, keepdims=True)
    terms = amount * jnp.exp(scores - top)
    total = jnp.sum(terms, axis=0, keepdims=True)
    adjoint = split(terms * (live_slot / total) - live_slot * tail_hot)
    dst_grad = three(nt, query, adjoint)
    back = three(nn, (dh[...], dl[...]), adjoint)
    b_re, b_im = back[:HALF], back[HALF:]
    to_head = split(jnp.concatenate([b_re * r_re + b_im * r_im, b_im * r_re - b_re * r_im], axis=0))
    src_grad = nt(to_head[0], head_hot) + nt(to_head[1], head_hot)
    flags = jnp.broadcast_to(live_slot, (16, SLOTS)).astype(jnp.bfloat16)
    head_count = nt(flags, head_hot)[0:1]
    tail_count = nt(flags, tail_hot.astype(jnp.bfloat16))[0:1]

    grads = []
    for rows, grad, times in ((src, src_grad, head_count), (dst, dst_grad, tail_count)):
        re, im = rows[:HALF], rows[HALF:]
        modulus = jnp.sqrt(re * re + im * im)
        pull = modulus * ((3.0 * cubic_weight) * times)
        grads.append((grad[:HALF] + pull * re, grad[HALF:] + pull * im))

    for t in range(4):
        at = slice(t * LANES, (t + 1) * LANES)
        tiles = exchange_lanes([grads[0][0][:, at], grads[1][0][:, at], grads[0][1][:, at], grads[1][1][:, at]])
        for g, tile in enumerate(tiles):
            p = 4 * t + g
            array, place = OUT_PLACE[p % 8]
            outs[array + 3 * (p // 8)][place] = tile


def table_kernel(columns, out_ref, came, goes, came_sems, goes_sems):
    depth, out_depth, width = came.shape[0], goes.shape[0], came.shape[2]
    parts = out_ref.shape[0] // width

    def fetch(i):
        at, slot = pl.multiple_of(i * width, width), lax.rem(i, depth)
        return pltpu.make_async_copy(columns.at[:, pl.ds(at, width)], came.at[slot], came_sems.at[slot])

    def store(i):
        at, slot = pl.multiple_of(i * width, width), lax.rem(i, out_depth)
        return pltpu.make_async_copy(goes.at[slot], out_ref.at[pl.ds(at, width), :], goes_sems.at[slot])

    for i in range(depth):
        fetch(jnp.int32(i)).start()

    def part(i, carry):
        fetch(i).wait()

        @pl.when(i >= out_depth)
        def _():
            store(i - out_depth).wait()

        goes[lax.rem(i, out_depth)] = came[lax.rem(i, depth)].T
        store(i).start()

        @pl.when(i + depth < parts)
        def _():
            fetch(i + depth).start()

        return carry

    lax.fori_loop(0, parts, part, 0)
    for i in range(parts - out_depth, parts):
        store(jnp.int32(i)).wait()


def by_rows(columns):
    width, count = columns.shape
    part = 2 * LANES
    return pl.pallas_call(
        table_kernel,
        out_shape=jax.ShapeDtypeStruct((count, width), jnp.float32),
        in_specs=[pl.BlockSpec(memory_space=pl.ANY)],
        out_specs=pl.BlockSpec(memory_space=pl.ANY),
        scratch_shapes=[
            pltpu.VMEM((8, width, part), jnp.float32),
            pltpu.VMEM((4, part, width), jnp.float32),
            pltpu.SemaphoreType.DMA((8,)),
            pltpu.SemaphoreType.DMA((4,)),
        ],
        compiler_params=pltpu.CompilerParams(vmem_limit_bytes=58 * MIB),
        cost_estimate=pl.CostEstimate(flops=0, bytes_accessed=27_000_000, transcendentals=0),
    )(columns)


def turns_kernel(ids, table, out_ref):
    def group(c, carry):
        rows = [table[pl.ds(ids[c // 8, (c % 8) * 16 + u], 1), :] for u in range(16)]
        for u, row in enumerate(rows):
            out_ref[pl.ds(c * 16 + u, 1), :] = row
        return carry

    lax.fori_loop(0, SLOTS // 16, group, 0)


def fetch_turns(table, ids):
    return pl.pallas_call(
        turns_kernel,
        out_shape=jax.ShapeDtypeStruct((SLOTS, table.shape[1]), jnp.float32),
        in_specs=[SMEM, VMEM],
        out_specs=VMEM,
        compiler_params=pltpu.CompilerParams(vmem_limit_bytes=4 * MIB),
        cost_estimate=pl.CostEstimate(flops=0, bytes_accessed=20_000_000, transcendentals=0),
    )(ids, table)


def step_grads(step, roster, arrived, drawn, blocks, turns):
    f32, bf16 = jnp.float32, jnp.bfloat16
    shapes = tuple(jax.ShapeDtypeStruct((n, HALF, LANES), f32) for n in (2, 2, 4))
    outs = pl.pallas_call(
        functools.partial(step_kernel, step, roster.shape[0]),
        out_shape=shapes * 2,
        in_specs=[SMEM] + [VMEM] * (3 + len(blocks)),
        out_specs=(VMEM,) * 6,
        scratch_shapes=[
            pltpu.VMEM((2 * HALF, PROWS), f32),
            pltpu.VMEM((2 * HALF, PROWS), f32),
            pltpu.VMEM((2 * HALF, PROWS), bf16),
            pltpu.VMEM((2 * HALF, PROWS), bf16),
            pltpu.VMEM((2 * HALF, PROWS), bf16),
            pltpu.VMEM((2 * HALF, PROWS), bf16),
            pltpu.VMEM((PROWS, 2 * HALF), bf16),
            pltpu.VMEM((PROWS, 2 * HALF), bf16),
        ],
        compiler_params=pltpu.CompilerParams(vmem_limit_bytes=20 * MIB),
        cost_estimate=pl.CostEstimate(flops=6_000_000_000, bytes_accessed=6_000_000, transcendentals=600_000),
    )(roster, arrived, drawn, *blocks, turns)
    return outs[:3], outs[3:]


def local(entity_table, adagrad_state, relations, roster, edge_triples, counts, negatives):
    my_dom = lax.axis_index("dom")
    steps, cap = edge_triples.shape[2], edge_triples.shape[3]
    devices = edge_triples.shape[1]

    edges = jnp.transpose(edge_triples[0], (1, 3, 2, 0)).reshape(steps * 3 * cap, devices)
    packed = jnp.concatenate(
        [edges, counts[0].T, jnp.zeros((LANES - steps * (3 * cap + 1), devices), jnp.int32)], axis=0
    ).T
    arrived = lax.all_to_all(packed, ("bucket", "dom"), split_axis=0, concat_axis=0, tiled=True).T

    rows = entity_table.reshape(2 * SHARD, 2 * HALF).T
    state = adagrad_state.reshape(1, 2 * SHARD)
    held = jnp.concatenate(
        [
            jnp.concatenate([rows[:HALF], rows[HALF:]], axis=1),
            jnp.broadcast_to(jnp.concatenate([state, state], axis=1), (8, LANES)),
        ],
        axis=0,
    )
    column = jnp.arange(PROWS, dtype=jnp.int32)
    roster = roster.reshape(steps, 16)

    def drawn(s):
        negs = place_dom(negatives[s, 0, 0], my_dom)
        return jnp.sum((negs[:, :, None] == column[None, None, :]).astype(jnp.float32), axis=1)

    def turns(s):
        base = s * 3 * cap + cap
        return fetch_turns(table, arrived[base:base + cap])

    arrived, (table,) = tied(arrived, by_rows(relations.T))
    brought, now_drawn, arrived = spread(held, bucket_perms(), drawn(0), arrived)
    now_turns = turns(0)
    for s in range(steps):
        x, st = select_blocks(brought, roster, s)
        now_turns, gathered = dom_gather(x, now_turns)
        own, other = step_grads(s, roster, arrived, now_drawn, gathered, now_turns)
        more = s + 1 < steps
        parts, now_turns, _ = dom_reduce(own, other, turns(s + 1) if more else None)
        held = adagrad(parts, x, st)
        brought, now_drawn, _ = spread(held, bucket_perms(), drawn(s + 1) if more else None)
    x, st = select_blocks(brought, roster, steps)
    rows = jnp.concatenate([x[:, :64], x[:, 64:]], axis=0).T.reshape(2, SHARD, 2 * HALF)
    return rows, st[0, :64].reshape(2, SHARD)


def solution(mesh):
    in_specs = (
        P("bucket", "dom", None),
        P("bucket", "dom"),
        P(),
        P(),
        P(("bucket", "dom"), None, None, None, None),
        P(("bucket", "dom"), None, None),
        P(None, "bucket", "dom", None, None),
    )
    out_specs = (P("bucket", "dom", None), P("bucket", "dom"))
    return jax.shard_map(local, mesh=mesh, in_specs=in_specs, out_specs=out_specs, check_vma=False)
```

profile of v0, /device:TPU:6, one launch (start us, length us, event | category | flops | bytes accessed | tf_op | source)
XLA Modules:
  0.0 319.5 jit_solution(15716424133542473301)
XLA Ops:
  5.2 2.3 convert_reduce_fusion.3.drawn
  7.8 4.0 %collective-permute-start.1 = (f32[416,128]{1,0:T(8,128)S(1)}, f32[416,128]{1,0:T(8,128)S(1)}, u32[]{:S(2)}, u32[]{:S(2)}) collective-permute-start(f32[416,128]{1,0:T(8,128)S(1)} %pad_maximum_fusion.refs_0_), channel_id=1, source_target_pairs={{0,64},{16,80},{32,96},{48,112},{64,0},{80,16},{96,32},{112,48},{1... | collective-permute-start | bytes 638984 | tf_op jit(solution)/shard_map/ppermute | solution.py:62
  16.6 6.8 %all-to-all-start = ((s32[128,1,128]{2,1,0:T(1,128)}), s32[128,1,128]{2,1,0:T(1,128)S(1)}, u32[]{:S(2)}, u32[]{:S(2)}) async-start(s32[128,1,128]{2,1,0:T(1,128)} %copy.64), calls=%async_computation | async-start | bytes 131072 | tf_op jit(solution)/shard_map/all_to_all | solution.py:398
  23.4 10.2 %shard_map.86.table = f32[7424,400]{1,0:T(8,128)} custom-call(f32[400,7424]{1,0:T(8,128)} %bitcast.95), custom_call_target="tpu_custom_call" | custom-call | bytes 27000000 | tf_op jit(solution)/shard_map/pallas_call | solution.py:328
  34.6 3.1 collective-permute-start.4
  37.7 5.3 %copy-done = f32[7424,400]{1,0:T(8,128)S(1)} copy-done((f32[7424,400]{1,0:T(8,128)S(1)}, f32[7424,400]{1,0:T(8,128)}, u32[]{:S(2)}) %copy-start) | copy-done | bytes 11878424
  43.0 5.9 %shard_map.88.refs_8_ = f32[1024,400]{1,0:T(8,128)S(1)} custom-call(s32[8,128]{1,0:T(8,128)S(1)} %get-tuple-element.149.ids, f32[7424,400]{1,0:T(8,128)S(1)} %copy-done), custom_call_target="tpu_custom_call" | custom-call | bytes 20000000 | tf_op jit(solution)/shard_map/pallas_call | solution.py:355
  53.1 8.4 %collective-permute-done.6.refs_2_ = f32[400,128]{1,0:T(8,128)S(1)} collective-permute-done((f32[400,128]{1,0:T(8,128)S(1)}, f32[400,128]{1,0:T(8,128)S(1)}, u32[]{:S(2)}, u32[]{:S(2)}) %collective-permute-start.6) | collective-permute-done | bytes 204832 | tf_op jit(solution)/shard_map/ppermute | solution.py:62
  63.8 9.8 %shard_map.89 = (f32[2,200,128]{2,1,0:T(8,128)S(1)}, f32[2,200,128]{2,1,0:T(8,128)S(1)}, f32[4,200,128]{2,1,0:T(8,128)S(1)}, f32[2,200,128]{2,1,0:T(8,128)S(1)},...) custom-call(s32[4,16]{1,0:T(4,128)S(1)} %copy.74.roster, s32[128,128]{1,0:T(8,128)S(1)} %bitcast.91, ...), custom_call_target="tpu_custom_call" | custom-call | flops 6000000000 | bytes 6000000 | tf_op jit(solution)/shard_map/pallas_call | solution.py:368
  75.1 2.7 collective-permute-start.16
  78.0 5.9 %shard_map.90.refs_8_ = f32[1024,400]{1,0:T(8,128)S(1)} custom-call(s32[8,128]{1,0:T(8,128)S(1)} %get-tuple-element.148.ids, f32[7424,400]{1,0:T(8,128)S(1)} %bitcast.89), custom_call_target="tpu_custom_call" | custom-call | bytes 20000000 | tf_op jit(solution)/shard_map/pallas_call | solution.py:355
  86.1 3.2 %collective-permute-start.17 = (f32[200,128]{1,0:T(8,128)S(1)}, f32[200,128]{1,0:T(8,128)S(1)}, u32[]{:S(2)}, u32[]{:S(2)}) collective-permute-start(f32[200,128]{1,0:T(8,128)S(1)} %get-tuple-element.80), channel_id=1, source_target_pairs={{0,2},{1,3},{2,4},{3,5},{4,6},{5,7},{6,0},{7,1},{8,10},{9,11},{10,... | collective-permute-start | bytes 307208 | tf_op jit(solution)/shard_map/ppermute | solution.py:84
  89.3 2.6 collective-permute-done.18
  92.6 5.6 %collective-permute-done.19.flipped = f32[200,128]{1,0:T(8,128)S(1)} collective-permute-done((f32[200,128]{1,0:T(8,128)S(1)}, f32[200,128]{1,0:T(8,128)S(1)}, u32[]{:S(2)}, u32[]{:S(2)}) %collective-permute-start.19) | collective-permute-done | bytes 102432 | tf_op jit(solution)/shard_map/ppermute | solution.py:84
  99.9 2.3 convert_reduce_fusion.2.drawn
  111.2 3.4 %collective-permute-done.23.refs_3_ = f32[416,128]{1,0:T(8,128)S(1)} collective-permute-done((f32[416,128]{1,0:T(8,128)S(1)}, f32[416,128]{1,0:T(8,128)S(1)}, u32[]{:S(2)}, u32[]{:S(2)}) %collective-permute-start.23) | collective-permute-done | bytes 213024 | tf_op jit(solution)/shard_map/ppermute | solution.py:62
  116.0 5.6 %collective-permute-done.24 = f32[200,128]{1,0:T(8,128)S(1)} collective-permute-done((f32[200,128]{1,0:T(8,128)S(1)}, f32[200,128]{1,0:T(8,128)S(1)}, u32[]{:S(2)}, u32[]{:S(2)}) %collective-permute-start.24) | collective-permute-done | bytes 102432 | tf_op jit(solution)/shard_map/ppermute | solution.py:62
  123.7 3.7 %collective-permute-done.25.refs_1_ = f32[400,128]{1,0:T(8,128)S(1)} collective-permute-done((f32[400,128]{1,0:T(8,128)S(1)}, f32[400,128]{1,0:T(8,128)S(1)}, u32[]{:S(2)}, u32[]{:S(2)}) %collective-permute-start.25) | collective-permute-done | bytes 204832 | tf_op jit(solution)/shard_map/ppermute | solution.py:62
  132.4 9.8 %shard_map.93 = (f32[2,200,128]{2,1,0:T(8,128)S(1)}, f32[2,200,128]{2,1,0:T(8,128)S(1)}, f32[4,200,128]{2,1,0:T(8,128)S(1)}, f32[2,200,128]{2,1,0:T(8,128)S(1)},...) custom-call(s32[4,16]{1,0:T(4,128)S(1)} %copy.74.roster, s32[128,128]{1,0:T(8,128)S(1)} %bitcast.92, ...), custom_call_target="tpu_custom_call" | custom-call | flops 6000000000 | bytes 6000000 | tf_op jit(solution)/shard_map/pallas_call | solution.py:368
  146.1 5.9 %shard_map.94.refs_8_ = f32[1024,400]{1,0:T(8,128)S(1)} custom-call(s32[8,128]{1,0:T(8,128)S(1)} %get-tuple-element.147.ids, f32[7424,400]{1,0:T(8,128)S(1)} %bitcast.89), custom_call_target="tpu_custom_call" | custom-call | bytes 20000000 | tf_op jit(solution)/shard_map/pallas_call | solution.py:355
  153.6 3.2 %collective-permute-start.37 = (f32[200,128]{1,0:T(8,128)S(1)}, f32[200,128]{1,0:T(8,128)S(1)}, u32[]{:S(2)}, u32[]{:S(2)}) collective-permute-start(f32[200,128]{1,0:T(8,128)S(1)} %get-tuple-element.95), channel_id=1, source_target_pairs={{0,2},{1,3},{2,4},{3,5},{4,6},{5,7},{6,0},{7,1},{8,10},{9,11},{10,... | collective-permute-start | bytes 307208 | tf_op jit(solution)/shard_map/ppermute | solution.py:84
  156.9 2.6 collective-permute-done.38
  160.2 5.6 %collective-permute-done.39.flipped = f32[200,128]{1,0:T(8,128)S(1)} collective-permute-done((f32[200,128]{1,0:T(8,128)S(1)}, f32[200,128]{1,0:T(8,128)S(1)}, u32[]{:S(2)}, u32[]{:S(2)}) %collective-permute-start.39) | collective-permute-done | bytes 102432 | tf_op jit(solution)/shard_map/ppermute | solution.py:84
  174.8 3.1 collective-permute-done.41.refs_1_
  178.1 3.2 %collective-permute-done.43.refs_3_ = f32[416,128]{1,0:T(8,128)S(1)} collective-permute-done((f32[416,128]{1,0:T(8,128)S(1)}, f32[416,128]{1,0:T(8,128)S(1)}, u32[]{:S(2)}, u32[]{:S(2)}) %collective-permute-start.43) | collective-permute-done | bytes 213024 | tf_op jit(solution)/shard_map/ppermute | solution.py:62
  182.8 5.6 %collective-permute-done.44 = f32[200,128]{1,0:T(8,128)S(1)} collective-permute-done((f32[200,128]{1,0:T(8,128)S(1)}, f32[200,128]{1,0:T(8,128)S(1)}, u32[]{:S(2)}, u32[]{:S(2)}) %collective-permute-start.44) | collective-permute-done | bytes 102432 | tf_op jit(solution)/shard_map/ppermute | solution.py:62
  190.6 3.6 %collective-permute-done.45.refs_1_ = f32[400,128]{1,0:T(8,128)S(1)} collective-permute-done((f32[400,128]{1,0:T(8,128)S(1)}, f32[400,128]{1,0:T(8,128)S(1)}, u32[]{:S(2)}, u32[]{:S(2)}) %collective-permute-start.45) | collective-permute-done | bytes 204832 | tf_op jit(solution)/shard_map/ppermute | solution.py:62
  194.2 3.8 %collective-permute-done.46.refs_2_ = f32[400,128]{1,0:T(8,128)S(1)} collective-permute-done((f32[400,128]{1,0:T(8,128)S(1)}, f32[400,128]{1,0:T(8,128)S(1)}, u32[]{:S(2)}, u32[]{:S(2)}) %collective-permute-start.46) | collective-permute-done | bytes 204832 | tf_op jit(solution)/shard_map/ppermute | solution.py:62
  199.8 9.8 %shard_map.97 = (f32[2,200,128]{2,1,0:T(8,128)S(1)}, f32[2,200,128]{2,1,0:T(8,128)S(1)}, f32[4,200,128]{2,1,0:T(8,128)S(1)}, f32[2,200,128]{2,1,0:T(8,128)S(1)},...) custom-call(s32[4,16]{1,0:T(4,128)S(1)} %copy.74.roster, s32[128,128]{1,0:T(8,128)S(1)} %bitcast.93, ...), custom_call_target="tpu_custom_call" | custom-call | flops 6000000000 | bytes 6000000 | tf_op jit(solution)/shard_map/pallas_call | solution.py:368
  213.4 5.9 %shard_map.98.refs_8_ = f32[1024,400]{1,0:T(8,128)S(1)} custom-call(s32[8,128]{1,0:T(8,128)S(1)} %get-tuple-element.146.ids, f32[7424,400]{1,0:T(8,128)S(1)} %bitcast.89), custom_call_target="tpu_custom_call" | custom-call | bytes 20000000 | tf_op jit(solution)/shard_map/pallas_call | solution.py:355
  220.8 3.2 %collective-permute-start.57 = (f32[200,128]{1,0:T(8,128)S(1)}, f32[200,128]{1,0:T(8,128)S(1)}, u32[]{:S(2)}, u32[]{:S(2)}) collective-permute-start(f32[200,128]{1,0:T(8,128)S(1)} %get-tuple-element.110), channel_id=1, source_target_pairs={{0,2},{1,3},{2,4},{3,5},{4,6},{5,7},{6,0},{7,1},{8,10},{9,11},{10,... | collective-permute-start | bytes 307208 | tf_op jit(solution)/shard_map/ppermute | solution.py:84
  224.0 2.6 collective-permute-done.58
  227.2 5.7 %collective-permute-done.59.flipped = f32[200,128]{1,0:T(8,128)S(1)} collective-permute-done((f32[200,128]{1,0:T(8,128)S(1)}, f32[200,128]{1,0:T(8,128)S(1)}, u32[]{:S(2)}, u32[]{:S(2)}) %collective-permute-start.59) | collective-permute-done | bytes 102432 | tf_op jit(solution)/shard_map/ppermute | solution.py:84
  233.1 2.4 collective-permute-start.60
  238.7 3.1 collective-permute-start.62
  242.0 3.6 %collective-permute-done.61.refs_1_ = f32[416,128]{1,0:T(8,128)S(1)} collective-permute-done((f32[416,128]{1,0:T(8,128)S(1)}, f32[416,128]{1,0:T(8,128)S(1)}, u32[]{:S(2)}, u32[]{:S(2)}) %collective-permute-start.61) | collective-permute-done | bytes 213024 | tf_op jit(solution)/shard_map/ppermute | solution.py:62
  250.3 5.8 %collective-permute-done.64 = f32[200,128]{1,0:T(8,128)S(1)} collective-permute-done((f32[200,128]{1,0:T(8,128)S(1)}, f32[200,128]{1,0:T(8,128)S(1)}, u32[]{:S(2)}, u32[]{:S(2)}) %collective-permute-start.64) | collective-permute-done | bytes 102432 | tf_op jit(solution)/shard_map/ppermute | solution.py:62
  258.2 3.7 %collective-permute-done.65.refs_1_ = f32[400,128]{1,0:T(8,128)S(1)} collective-permute-done((f32[400,128]{1,0:T(8,128)S(1)}, f32[400,128]{1,0:T(8,128)S(1)}, u32[]{:S(2)}, u32[]{:S(2)}) %collective-permute-start.65) | collective-permute-done | bytes 204832 | tf_op jit(solution)/shard_map/ppermute | solution.py:62
  262.0 3.9 %collective-permute-done.66.refs_2_ = f32[400,128]{1,0:T(8,128)S(1)} collective-permute-done((f32[400,128]{1,0:T(8,128)S(1)}, f32[400,128]{1,0:T(8,128)S(1)}, u32[]{:S(2)}, u32[]{:S(2)}) %collective-permute-start.66) | collective-permute-done | bytes 204832 | tf_op jit(solution)/shard_map/ppermute | solution.py:62
  267.6 9.8 %shard_map.101 = (f32[2,200,128]{2,1,0:T(8,128)S(1)}, f32[2,200,128]{2,1,0:T(8,128)S(1)}, f32[4,200,128]{2,1,0:T(8,128)S(1)}, f32[2,200,128]{2,1,0:T(8,128)S(1)}...) custom-call(s32[4,16]{1,0:T(4,128)S(1)} %copy.74.roster, s32[128,128]{1,0:T(8,128)S(1)} %bitcast.94, ...), custom_call_target="tpu_custom_call" | custom-call | flops 6000000000 | bytes 6000000 | tf_op jit(solution)/shard_map/pallas_call | solution.py:368
  281.4 5.1 %collective-permute-done.76 = f32[2,200,128]{2,1,0:T(8,128)S(1)} collective-permute-done((f32[2,200,128]{2,1,0:T(8,128)S(1)}, f32[2,200,128]{2,1,0:T(8,128)S(1)}, u32[]{:S(2)}, u32[]{:S(2)}) %collective-permute-start.76) | collective-permute-done | bytes 204832 | tf_op jit(solution)/shard_map/ppermute | solution.py:84
  288.6 3.2 %collective-permute-start.77 = (f32[200,128]{1,0:T(8,128)S(1)}, f32[200,128]{1,0:T(8,128)S(1)}, u32[]{:S(2)}, u32[]{:S(2)}) collective-permute-start(f32[200,128]{1,0:T(8,128)S(1)} %get-tuple-element.131), channel_id=1, source_target_pairs={{0,2},{1,3},{2,4},{3,5},{4,6},{5,7},{6,0},{7,1},{8,10},{9,11},{10,... | collective-permute-start | bytes 307208 | tf_op jit(solution)/shard_map/ppermute | solution.py:84
  291.9 2.6 collective-permute-done.78
  295.0 5.8 %collective-permute-done.79.flipped = f32[200,128]{1,0:T(8,128)S(1)} collective-permute-done((f32[200,128]{1,0:T(8,128)S(1)}, f32[200,128]{1,0:T(8,128)S(1)}, u32[]{:S(2)}, u32[]{:S(2)}) %collective-permute-start.79) | collective-permute-done | bytes 102432 | tf_op jit(solution)/shard_map/ppermute | solution.py:84
  300.9 2.4 collective-permute-start.80
  303.4 2.7 collective-permute-done.80
  306.5 2.9 collective-permute-start.82
  309.5 3.6 %collective-permute-done.81.refs_1_ = f32[416,128]{1,0:T(8,128)S(1)} collective-permute-done((f32[416,128]{1,0:T(8,128)S(1)}, f32[416,128]{1,0:T(8,128)S(1)}, u32[]{:S(2)}, u32[]{:S(2)}) %collective-permute-start.81) | collective-permute-done | bytes 213024 | tf_op jit(solution)/shard_map/ppermute | solution.py:62
  (206 shorter events, 92.6 us)
Async XLA Ops:
  7.8 26.1 %collective-permute-start.1 = (f32[416,128]{1,0:T(8,128)S(1)}, f32[416,128]{1,0:T(8,128)S(1)}, u32[]{:S(2)}, u32[]{:S(2)}) collective-permute-start(f32[416,128]{1,0:T(8,128)S(1)} %pad_maximum_fusion.refs_0_), channel_id=1, source_target_pairs={{0,64},{16,80},{32,96},{48,112},{64,0},{80,16},{96,32},{112,48},{1... | collective-permute-start | bytes 638984 | tf_op jit(solution)/shard_map/ppermute | solution.py:62
  11.7 22.1 %collective-permute-start.2 = (f32[416,128]{1,0:T(8,128)S(1)}, f32[416,128]{1,0:T(8,128)S(1)}, u32[]{:S(2)}, u32[]{:S(2)}) collective-permute-start(f32[416,128]{1,0:T(8,128)S(1)} %pad_maximum_fusion.refs_0_), channel_id=1, source_target_pairs={{0,32},{16,48},{32,64},{48,80},{64,96},{80,112},{96,0},{112,16},{1... | collective-permute-start | bytes 638984 | tf_op jit(solution)/shard_map/ppermute | solution.py:62
  12.7 21.1 %collective-permute-start.3 = (f32[416,128]{1,0:T(8,128)S(1)}, f32[416,128]{1,0:T(8,128)S(1)}, u32[]{:S(2)}, u32[]{:S(2)}) collective-permute-start(f32[416,128]{1,0:T(8,128)S(1)} %pad_maximum_fusion.refs_0_), channel_id=1, source_target_pairs={{0,96},{16,112},{32,0},{48,16},{64,32},{80,48},{96,64},{112,80},{1... | collective-permute-start | bytes 638984 | tf_op jit(solution)/shard_map/ppermute | solution.py:62
  16.6 17.2 %all-to-all-start = ((s32[128,1,128]{2,1,0:T(1,128)}), s32[128,1,128]{2,1,0:T(1,128)S(1)}, u32[]{:S(2)}, u32[]{:S(2)}) async-start(s32[128,1,128]{2,1,0:T(1,128)} %copy.64), calls=%async_computation | async-start | bytes 131072 | tf_op jit(solution)/shard_map/all_to_all | solution.py:398
  34.6 14.3 %collective-permute-start.4 = (f32[200,128]{1,0:T(8,128)S(1)}, f32[200,128]{1,0:T(8,128)S(1)}, u32[]{:S(2)}, u32[]{:S(2)}) collective-permute-start(f32[200,128]{1,0:T(8,128)S(1)} %get-tuple-element.70.x_ref), channel_id=1, source_target_pairs={{0,8},{1,9},{2,10},{3,11},{4,12},{5,13},{6,14},{7,15},{8,0},{9,1},... | collective-permute-start | bytes 307208 | tf_op jit(solution)/shard_map/ppermute | solution.py:62
  49.0 12.5 %collective-permute-start.6 = (f32[400,128]{1,0:T(8,128)S(1)}, f32[400,128]{1,0:T(8,128)S(1)}, u32[]{:S(2)}, u32[]{:S(2)}) collective-permute-start(f32[400,128]{1,0:T(8,128)S(1)} %constant_dynamic-update-slice_fusion.refs_0_), channel_id=1, source_target_pairs={{0,6},{1,7},{2,0},{3,1},{4,2},{5,3},{6,4},{7,5},{8,14},{9,15},{10,... | collective-permute-start | bytes 614408 | tf_op jit(solution)/shard_map/ppermute | solution.py:62
  49.9 11.6 %collective-permute-start.7 = (f32[400,128]{1,0:T(8,128)S(1)}, f32[400,128]{1,0:T(8,128)S(1)}, u32[]{:S(2)}, u32[]{:S(2)}) collective-permute-start(f32[400,128]{1,0:T(8,128)S(1)} %constant_dynamic-update-slice_fusion.refs_0_), channel_id=1, source_target_pairs={{0,4},{1,5},{2,6},{3,7},{4,0},{5,1},{6,2},{7,3},{8,12},{9,13},{10,... | collective-permute-start | bytes 614408 | tf_op jit(solution)/shard_map/ppermute | solution.py:62
  51.1 11.1 %collective-permute-start.5 = (f32[400,128]{1,0:T(8,128)S(1)}, f32[400,128]{1,0:T(8,128)S(1)}, u32[]{:S(2)}, u32[]{:S(2)}) collective-permute-start(f32[400,128]{1,0:T(8,128)S(1)} %constant_dynamic-update-slice_fusion.refs_0_), channel_id=1, source_target_pairs={{0,2},{1,3},{2,4},{3,5},{4,6},{5,7},{6,0},{7,1},{8,10},{9,11},{10,... | collective-permute-start | bytes 614408 | tf_op jit(solution)/shard_map/ppermute | solution.py:62
  53.1 9.2 %collective-permute-start.8 = (f32[400,128]{1,0:T(8,128)S(1)}, f32[400,128]{1,0:T(8,128)S(1)}, u32[]{:S(2)}, u32[]{:S(2)}) collective-permute-start(f32[400,128]{1,0:T(8,128)S(1)} %constant_dynamic-update-slice_fusion.refs_0_), channel_id=1, source_target_pairs={{0,1},{1,0},{2,3},{3,2},{4,5},{5,4},{6,7},{7,6},{8,9},{9,8},{10,11... | collective-permute-start | bytes 614408 | tf_op jit(solution)/shard_map/ppermute | solution.py:77
  74.2 11.8 %collective-permute-start.12 = (f32[4,200,128]{2,1,0:T(8,128)S(1)}, f32[4,200,128]{2,1,0:T(8,128)S(1)}, u32[]{:S(2)}, u32[]{:S(2)}) collective-permute-start(f32[4,200,128]{2,1,0:T(8,128)S(1)} %get-tuple-element.75), channel_id=1, source_target_pairs={{0,1},{1,0},{2,3},{3,2},{4,5},{5,4},{6,7},{7,6},{8,9},{9,8},{10,11... | collective-permute-start | bytes 1228808 | tf_op jit(solution)/shard_map/ppermute | solution.py:84
  75.1 8.8 %collective-permute-start.16 = (f32[2,200,128]{2,1,0:T(8,128)S(1)}, f32[2,200,128]{2,1,0:T(8,128)S(1)}, u32[]{:S(2)}, u32[]{:S(2)}) collective-permute-start(f32[2,200,128]{2,1,0:T(8,128)S(1)} %add.241), channel_id=1, source_target_pairs={{0,2},{1,3},{2,4},{3,5},{4,6},{5,7},{6,0},{7,1},{8,10},{9,11},{10,... | collective-permute-start | bytes 614408 | tf_op jit(solution)/shard_map/ppermute | solution.py:84
  77.8 8.1 %collective-permute-start.14 = (f32[2,200,128]{2,1,0:T(8,128)S(1)}, f32[2,200,128]{2,1,0:T(8,128)S(1)}, u32[]{:S(2)}, u32[]{:S(2)}) collective-permute-start(f32[2,200,128]{2,1,0:T(8,128)S(1)} %add.239), channel_id=1, source_target_pairs={{0,6},{1,7},{2,0},{3,1},{4,2},{5,3},{6,4},{7,5},{8,14},{9,15},{10,... | collective-permute-start | bytes 614408 | tf_op jit(solution)/shard_map/ppermute | solution.py:84
  86.1 6.5 %collective-permute-start.17 = (f32[200,128]{1,0:T(8,128)S(1)}, f32[200,128]{1,0:T(8,128)S(1)}, u32[]{:S(2)}, u32[]{:S(2)}) collective-permute-start(f32[200,128]{1,0:T(8,128)S(1)} %get-tuple-element.80), channel_id=1, source_target_pairs={{0,2},{1,3},{2,4},{3,5},{4,6},{5,7},{6,0},{7,1},{8,10},{9,11},{10,... | collective-permute-start | bytes 307208 | tf_op jit(solution)/shard_map/ppermute | solution.py:84
  92.0 6.2 %collective-permute-start.19 = (f32[200,128]{1,0:T(8,128)S(1)}, f32[200,128]{1,0:T(8,128)S(1)}, u32[]{:S(2)}, u32[]{:S(2)}) collective-permute-start(f32[200,128]{1,0:T(8,128)S(1)} %fusion.16), channel_id=1, source_target_pairs={{0,8},{1,9},{2,10},{3,11},{4,12},{5,13},{6,14},{7,15},{8,0},{9,1},... | collective-permute-start | bytes 307208 | tf_op jit(solution)/shard_map/ppermute | solution.py:84
  103.2 8.0 %collective-permute-start.21 = (f32[416,128]{1,0:T(8,128)S(1)}, f32[416,128]{1,0:T(8,128)S(1)}, u32[]{:S(2)}, u32[]{:S(2)}) collective-permute-start(f32[416,128]{1,0:T(8,128)S(1)} %pad_maximum_fusion.1.refs_0_), channel_id=1, source_target_pairs={{0,32},{16,48},{32,64},{48,80},{64,96},{80,112},{96,0},{112,16},{1... | collective-permute-start | bytes 638984 | tf_op jit(solution)/shard_map/ppermute | solution.py:62
  107.2 7.3 %collective-permute-start.23 = (f32[416,128]{1,0:T(8,128)S(1)}, f32[416,128]{1,0:T(8,128)S(1)}, u32[]{:S(2)}, u32[]{:S(2)}) collective-permute-start(f32[416,128]{1,0:T(8,128)S(1)} %pad_maximum_fusion.1.refs_0_), channel_id=1, source_target_pairs={{0,64},{16,80},{32,96},{48,112},{64,0},{80,16},{96,32},{112,48},{1... | collective-permute-start | bytes 638984 | tf_op jit(solution)/shard_map/ppermute | solution.py:62
  115.3 6.2 %collective-permute-start.24 = (f32[200,128]{1,0:T(8,128)S(1)}, f32[200,128]{1,0:T(8,128)S(1)}, u32[]{:S(2)}, u32[]{:S(2)}) collective-permute-start(f32[200,128]{1,0:T(8,128)S(1)} %get-tuple-element.85.x_ref), channel_id=1, source_target_pairs={{0,8},{1,9},{2,10},{3,11},{4,12},{5,13},{6,14},{7,15},{8,0},{9,1},... | collective-permute-start | bytes 307208 | tf_op jit(solution)/shard_map/ppermute | solution.py:62
  121.7 7.0 %collective-permute-start.26 = (f32[400,128]{1,0:T(8,128)S(1)}, f32[400,128]{1,0:T(8,128)S(1)}, u32[]{:S(2)}, u32[]{:S(2)}) collective-permute-start(f32[400,128]{1,0:T(8,128)S(1)} %constant_dynamic-update-slice_fusion.2.refs_0_), channel_id=1, source_target_pairs={{0,6},{1,7},{2,0},{3,1},{4,2},{5,3},{6,4},{7,5},{8,14},{9,15},{10,... | collective-permute-start | bytes 614408 | tf_op jit(solution)/shard_map/ppermute | solution.py:62
  123.7 7.3 %collective-permute-start.27 = (f32[400,128]{1,0:T(8,128)S(1)}, f32[400,128]{1,0:T(8,128)S(1)}, u32[]{:S(2)}, u32[]{:S(2)}) collective-permute-start(f32[400,128]{1,0:T(8,128)S(1)} %constant_dynamic-update-slice_fusion.2.refs_0_), channel_id=1, source_target_pairs={{0,4},{1,5},{2,6},{3,7},{4,0},{5,1},{6,2},{7,3},{8,12},{9,13},{10,... | collective-permute-start | bytes 614408 | tf_op jit(solution)/shard_map/ppermute | solution.py:62
  123.7 7.3 %collective-permute-start.28 = (f32[400,128]{1,0:T(8,128)S(1)}, f32[400,128]{1,0:T(8,128)S(1)}, u32[]{:S(2)}, u32[]{:S(2)}) collective-permute-start(f32[400,128]{1,0:T(8,128)S(1)} %constant_dynamic-update-slice_fusion.2.refs_0_), channel_id=1, source_target_pairs={{0,1},{1,0},{2,3},{3,2},{4,5},{5,4},{6,7},{7,6},{8,9},{9,8},{10,11... | collective-permute-start | bytes 614408 | tf_op jit(solution)/shard_map/ppermute | solution.py:77
  142.8 10.7 %collective-permute-start.32 = (f32[4,200,128]{2,1,0:T(8,128)S(1)}, f32[4,200,128]{2,1,0:T(8,128)S(1)}, u32[]{:S(2)}, u32[]{:S(2)}) collective-permute-start(f32[4,200,128]{2,1,0:T(8,128)S(1)} %get-tuple-element.90), channel_id=1, source_target_pairs={{0,1},{1,0},{2,3},{3,2},{4,5},{5,4},{6,7},{7,6},{8,9},{9,8},{10,11... | collective-permute-start | bytes 1228808 | tf_op jit(solution)/shard_map/ppermute | solution.py:84
  143.8 8.3 %collective-permute-start.36 = (f32[2,200,128]{2,1,0:T(8,128)S(1)}, f32[2,200,128]{2,1,0:T(8,128)S(1)}, u32[]{:S(2)}, u32[]{:S(2)}) collective-permute-start(f32[2,200,128]{2,1,0:T(8,128)S(1)} %add.256), channel_id=1, source_target_pairs={{0,2},{1,3},{2,4},{3,5},{4,6},{5,7},{6,0},{7,1},{8,10},{9,11},{10,... | collective-permute-start | bytes 614408 | tf_op jit(solution)/shard_map/ppermute | solution.py:84
  145.2 8.3 %collective-permute-start.34 = (f32[2,200,128]{2,1,0:T(8,128)S(1)}, f32[2,200,128]{2,1,0:T(8,128)S(1)}, u32[]{:S(2)}, u32[]{:S(2)}) collective-permute-start(f32[2,200,128]{2,1,0:T(8,128)S(1)} %add.254), channel_id=1, source_target_pairs={{0,6},{1,7},{2,0},{3,1},{4,2},{5,3},{6,4},{7,5},{8,14},{9,15},{10,... | collective-permute-start | bytes 614408 | tf_op jit(solution)/shard_map/ppermute | solution.py:84
  153.6 6.5 %collective-permute-start.37 = (f32[200,128]{1,0:T(8,128)S(1)}, f32[200,128]{1,0:T(8,128)S(1)}, u32[]{:S(2)}, u32[]{:S(2)}) collective-permute-start(f32[200,128]{1,0:T(8,128)S(1)} %get-tuple-element.95), channel_id=1, source_target_pairs={{0,2},{1,3},{2,4},{3,5},{4,6},{5,7},{6,0},{7,1},{8,10},{9,11},{10,... | collective-permute-start | bytes 307208 | tf_op jit(solution)/shard_map/ppermute | solution.py:84
  170.7 7.1 %collective-permute-start.41 = (f32[416,128]{1,0:T(8,128)S(1)}, f32[416,128]{1,0:T(8,128)S(1)}, u32[]{:S(2)}, u32[]{:S(2)}) collective-permute-start(f32[416,128]{1,0:T(8,128)S(1)} %pad_maximum_fusion.2.refs_0_), channel_id=1, source_target_pairs={{0,32},{16,48},{32,64},{48,80},{64,96},{80,112},{96,0},{112,16},{1... | collective-permute-start | bytes 638984 | tf_op jit(solution)/shard_map/ppermute | solution.py:62
  174.0 7.3 %collective-permute-start.43 = (f32[416,128]{1,0:T(8,128)S(1)}, f32[416,128]{1,0:T(8,128)S(1)}, u32[]{:S(2)}, u32[]{:S(2)}) collective-permute-start(f32[416,128]{1,0:T(8,128)S(1)} %pad_maximum_fusion.2.refs_0_), channel_id=1, source_target_pairs={{0,64},{16,80},{32,96},{48,112},{64,0},{80,16},{96,32},{112,48},{1... | collective-permute-start | bytes 638984 | tf_op jit(solution)/shard_map/ppermute | solution.py:62
  188.9 9.2 %collective-permute-start.46 = (f32[400,128]{1,0:T(8,128)S(1)}, f32[400,128]{1,0:T(8,128)S(1)}, u32[]{:S(2)}, u32[]{:S(2)}) collective-permute-start(f32[400,128]{1,0:T(8,128)S(1)} %constant_dynamic-update-slice_fusion.4.refs_0_), channel_id=1, source_target_pairs={{0,6},{1,7},{2,0},{3,1},{4,2},{5,3},{6,4},{7,5},{8,14},{9,15},{10,... | collective-permute-start | bytes 614408 | tf_op jit(solution)/shard_map/ppermute | solution.py:62
  190.5 7.6 %collective-permute-start.47 = (f32[400,128]{1,0:T(8,128)S(1)}, f32[400,128]{1,0:T(8,128)S(1)}, u32[]{:S(2)}, u32[]{:S(2)}) collective-permute-start(f32[400,128]{1,0:T(8,128)S(1)} %constant_dynamic-update-slice_fusion.4.refs_0_), channel_id=1, source_target_pairs={{0,4},{1,5},{2,6},{3,7},{4,0},{5,1},{6,2},{7,3},{8,12},{9,13},{10,... | collective-permute-start | bytes 614408 | tf_op jit(solution)/shard_map/ppermute | solution.py:62
  190.6 8.2 %collective-permute-start.48 = (f32[400,128]{1,0:T(8,128)S(1)}, f32[400,128]{1,0:T(8,128)S(1)}, u32[]{:S(2)}, u32[]{:S(2)}) collective-permute-start(f32[400,128]{1,0:T(8,128)S(1)} %constant_dynamic-update-slice_fusion.4.refs_0_), channel_id=1, source_target_pairs={{0,1},{1,0},{2,3},{3,2},{4,5},{5,4},{6,7},{7,6},{8,9},{9,8},{10,11... | collective-permute-start | bytes 614408 | tf_op jit(solution)/shard_map/ppermute | solution.py:77
  210.2 10.4 %collective-permute-start.52 = (f32[4,200,128]{2,1,0:T(8,128)S(1)}, f32[4,200,128]{2,1,0:T(8,128)S(1)}, u32[]{:S(2)}, u32[]{:S(2)}) collective-permute-start(f32[4,200,128]{2,1,0:T(8,128)S(1)} %get-tuple-element.105), channel_id=1, source_target_pairs={{0,1},{1,0},{2,3},{3,2},{4,5},{5,4},{6,7},{7,6},{8,9},{9,8},{10,11... | collective-permute-start | bytes 1228808 | tf_op jit(solution)/shard_map/ppermute | solution.py:84
  211.2 8.1 %collective-permute-start.56 = (f32[2,200,128]{2,1,0:T(8,128)S(1)}, f32[2,200,128]{2,1,0:T(8,128)S(1)}, u32[]{:S(2)}, u32[]{:S(2)}) collective-permute-start(f32[2,200,128]{2,1,0:T(8,128)S(1)} %add.271), channel_id=1, source_target_pairs={{0,2},{1,3},{2,4},{3,5},{4,6},{5,7},{6,0},{7,1},{8,10},{9,11},{10,... | collective-permute-start | bytes 614408 | tf_op jit(solution)/shard_map/ppermute | solution.py:84
  212.5 8.1 %collective-permute-start.54 = (f32[2,200,128]{2,1,0:T(8,128)S(1)}, f32[2,200,128]{2,1,0:T(8,128)S(1)}, u32[]{:S(2)}, u32[]{:S(2)}) collective-permute-start(f32[2,200,128]{2,1,0:T(8,128)S(1)} %add.269), channel_id=1, source_target_pairs={{0,6},{1,7},{2,0},{3,1},{4,2},{5,3},{6,4},{7,5},{8,14},{9,15},{10,... | collective-permute-start | bytes 614408 | tf_op jit(solution)/shard_map/ppermute | solution.py:84
  220.8 6.5 %collective-permute-start.57 = (f32[200,128]{1,0:T(8,128)S(1)}, f32[200,128]{1,0:T(8,128)S(1)}, u32[]{:S(2)}, u32[]{:S(2)}) collective-permute-start(f32[200,128]{1,0:T(8,128)S(1)} %get-tuple-element.110), channel_id=1, source_target_pairs={{0,2},{1,3},{2,4},{3,5},{4,6},{5,7},{6,0},{7,1},{8,10},{9,11},{10,... | collective-permute-start | bytes 307208 | tf_op jit(solution)/shard_map/ppermute | solution.py:84
  238.2 7.5 %collective-permute-start.61 = (f32[416,128]{1,0:T(8,128)S(1)}, f32[416,128]{1,0:T(8,128)S(1)}, u32[]{:S(2)}, u32[]{:S(2)}) collective-permute-start(f32[416,128]{1,0:T(8,128)S(1)} %pad_maximum_fusion.3.refs_0_), channel_id=1, source_target_pairs={{0,32},{16,48},{32,64},{48,80},{64,96},{80,112},{96,0},{112,16},{1... | collective-permute-start | bytes 638984 | tf_op jit(solution)/shard_map/ppermute | solution.py:62
  238.7 8.8 %collective-permute-start.62 = (f32[416,128]{1,0:T(8,128)S(1)}, f32[416,128]{1,0:T(8,128)S(1)}, u32[]{:S(2)}, u32[]{:S(2)}) collective-permute-start(f32[416,128]{1,0:T(8,128)S(1)} %pad_maximum_fusion.3.refs_0_), channel_id=1, source_target_pairs={{0,96},{16,112},{32,0},{48,16},{64,32},{80,48},{96,64},{112,80},{1... | collective-permute-start | bytes 638984 | tf_op jit(solution)/shard_map/ppermute | solution.py:62
  241.8 7.3 %collective-permute-start.63 = (f32[416,128]{1,0:T(8,128)S(1)}, f32[416,128]{1,0:T(8,128)S(1)}, u32[]{:S(2)}, u32[]{:S(2)}) collective-permute-start(f32[416,128]{1,0:T(8,128)S(1)} %pad_maximum_fusion.3.refs_0_), channel_id=1, source_target_pairs={{0,64},{16,80},{32,96},{48,112},{64,0},{80,16},{96,32},{112,48},{1... | collective-permute-start | bytes 638984 | tf_op jit(solution)/shard_map/ppermute | solution.py:62
  249.9 6.2 %collective-permute-start.64 = (f32[200,128]{1,0:T(8,128)S(1)}, f32[200,128]{1,0:T(8,128)S(1)}, u32[]{:S(2)}, u32[]{:S(2)}) collective-permute-start(f32[200,128]{1,0:T(8,128)S(1)} %get-tuple-element.115.x_ref), channel_id=1, source_target_pairs={{0,8},{1,9},{2,10},{3,11},{4,12},{5,13},{6,14},{7,15},{8,0},{9,1},... | collective-permute-start | bytes 307208 | tf_op jit(solution)/shard_map/ppermute | solution.py:62
  256.7 9.2 %collective-permute-start.66 = (f32[400,128]{1,0:T(8,128)S(1)}, f32[400,128]{1,0:T(8,128)S(1)}, u32[]{:S(2)}, u32[]{:S(2)}) collective-permute-start(f32[400,128]{1,0:T(8,128)S(1)} %constant_dynamic-update-slice_fusion.6.refs_0_), channel_id=1, source_target_pairs={{0,6},{1,7},{2,0},{3,1},{4,2},{5,3},{6,4},{7,5},{8,14},{9,15},{10,... | collective-permute-start | bytes 614408 | tf_op jit(solution)/shard_map/ppermute | solution.py:62
  258.2 7.6 %collective-permute-start.67 = (f32[400,128]{1,0:T(8,128)S(1)}, f32[400,128]{1,0:T(8,128)S(1)}, u32[]{:S(2)}, u32[]{:S(2)}) collective-permute-start(f32[400,128]{1,0:T(8,128)S(1)} %constant_dynamic-update-slice_fusion.6.refs_0_), channel_id=1, source_target_pairs={{0,4},{1,5},{2,6},{3,7},{4,0},{5,1},{6,2},{7,3},{8,12},{9,13},{10,... | collective-permute-start | bytes 614408 | tf_op jit(solution)/shard_map/ppermute | solution.py:62
  258.2 8.1 %collective-permute-start.68 = (f32[400,128]{1,0:T(8,128)S(1)}, f32[400,128]{1,0:T(8,128)S(1)}, u32[]{:S(2)}, u32[]{:S(2)}) collective-permute-start(f32[400,128]{1,0:T(8,128)S(1)} %constant_dynamic-update-slice_fusion.6.refs_0_), channel_id=1, source_target_pairs={{0,1},{1,0},{2,3},{3,2},{4,5},{5,4},{6,7},{7,6},{8,9},{9,8},{10,11... | collective-permute-start | bytes 614408 | tf_op jit(solution)/shard_map/ppermute | solution.py:77
  278.0 10.5 %collective-permute-start.72 = (f32[4,200,128]{2,1,0:T(8,128)S(1)}, f32[4,200,128]{2,1,0:T(8,128)S(1)}, u32[]{:S(2)}, u32[]{:S(2)}) collective-permute-start(f32[4,200,128]{2,1,0:T(8,128)S(1)} %get-tuple-element.120), channel_id=1, source_target_pairs={{0,1},{1,0},{2,3},{3,2},{4,5},{5,4},{6,7},{7,6},{8,9},{9,8},{10,11... | collective-permute-start | bytes 1228808 | tf_op jit(solution)/shard_map/ppermute | solution.py:84
  279.0 7.6 %collective-permute-start.76 = (f32[2,200,128]{2,1,0:T(8,128)S(1)}, f32[2,200,128]{2,1,0:T(8,128)S(1)}, u32[]{:S(2)}, u32[]{:S(2)}) collective-permute-start(f32[2,200,128]{2,1,0:T(8,128)S(1)} %add.286), channel_id=1, source_target_pairs={{0,2},{1,3},{2,4},{3,5},{4,6},{5,7},{6,0},{7,1},{8,10},{9,11},{10,... | collective-permute-start | bytes 614408 | tf_op jit(solution)/shard_map/ppermute | solution.py:84
  280.4 8.1 %collective-permute-start.74 = (f32[2,200,128]{2,1,0:T(8,128)S(1)}, f32[2,200,128]{2,1,0:T(8,128)S(1)}, u32[]{:S(2)}, u32[]{:S(2)}) collective-permute-start(f32[2,200,128]{2,1,0:T(8,128)S(1)} %add.284), channel_id=1, source_target_pairs={{0,6},{1,7},{2,0},{3,1},{4,2},{5,3},{6,4},{7,5},{8,14},{9,15},{10,... | collective-permute-start | bytes 614408 | tf_op jit(solution)/shard_map/ppermute | solution.py:84
  288.6 6.3 %collective-permute-start.77 = (f32[200,128]{1,0:T(8,128)S(1)}, f32[200,128]{1,0:T(8,128)S(1)}, u32[]{:S(2)}, u32[]{:S(2)}) collective-permute-start(f32[200,128]{1,0:T(8,128)S(1)} %get-tuple-element.131), channel_id=1, source_target_pairs={{0,2},{1,3},{2,4},{3,5},{4,6},{5,7},{6,0},{7,1},{8,10},{9,11},{10,... | collective-permute-start | bytes 307208 | tf_op jit(solution)/shard_map/ppermute | solution.py:84
  294.5 6.2 %collective-permute-start.79 = (f32[200,128]{1,0:T(8,128)S(1)}, f32[200,128]{1,0:T(8,128)S(1)}, u32[]{:S(2)}, u32[]{:S(2)}) collective-permute-start(f32[200,128]{1,0:T(8,128)S(1)} %fusion.2), channel_id=1, source_target_pairs={{0,8},{1,9},{2,10},{3,11},{4,12},{5,13},{6,14},{7,15},{8,0},{9,1},... | collective-permute-start | bytes 307208 | tf_op jit(solution)/shard_map/ppermute | solution.py:84
  306.1 7.1 %collective-permute-start.81 = (f32[416,128]{1,0:T(8,128)S(1)}, f32[416,128]{1,0:T(8,128)S(1)}, u32[]{:S(2)}, u32[]{:S(2)}) collective-permute-start(f32[416,128]{1,0:T(8,128)S(1)} %pad_maximum_fusion.4.refs_0_), channel_id=1, source_target_pairs={{0,32},{16,48},{32,64},{48,80},{64,96},{80,112},{96,0},{112,16},{1... | collective-permute-start | bytes 638984 | tf_op jit(solution)/shard_map/ppermute | solution.py:62
  306.5 8.6 %collective-permute-start.82 = (f32[416,128]{1,0:T(8,128)S(1)}, f32[416,128]{1,0:T(8,128)S(1)}, u32[]{:S(2)}, u32[]{:S(2)}) collective-permute-start(f32[416,128]{1,0:T(8,128)S(1)} %pad_maximum_fusion.4.refs_0_), channel_id=1, source_target_pairs={{0,96},{16,112},{32,0},{48,16},{64,32},{80,48},{96,64},{112,80},{1... | collective-permute-start | bytes 638984 | tf_op jit(solution)/shard_map/ppermute | solution.py:62
  309.4 7.3 %collective-permute-start.83 = (f32[416,128]{1,0:T(8,128)S(1)}, f32[416,128]{1,0:T(8,128)S(1)}, u32[]{:S(2)}, u32[]{:S(2)}) collective-permute-start(f32[416,128]{1,0:T(8,128)S(1)} %pad_maximum_fusion.4.refs_0_), channel_id=1, source_target_pairs={{0,64},{16,80},{32,96},{48,112},{64,0},{80,16},{96,32},{112,48},{1... | collective-permute-start | bytes 638984 | tf_op jit(solution)/shard_map/ppermute | solution.py:62
  (43 other events, 308.3 us)
where the time goes:
time: 325 us; the launch traced here: 320 us
  waiting for transfers between devices  132 us (41%)
  starting transfers between devices  87.2 us (27%)
  Pallas kernels  77.2 us (24%)
  other arithmetic  11.9 us (4%)
  local copies, waits for them, and re-layouts  9.82 us (3%)
    ppermute x36, waiting for transfers between devices, go(): return lax.ppermute(v, perms['axis'], perms[name])  78.4 us
    ppermute x36, starting transfers between devices, go(): return lax.ppermute(v, perms['axis'], perms[name])  50 us
    ppermute x32, waiting for transfers between devices, go(): return lax.ppermute(v, 'dom', perms[name])  48.1 us
    pallas_call x4, Pallas kernels, step_grads(): pl.pallas_call(functools.partial(step_kernel, step, roster.shape[0]), out...  39.2 us
    ppermute x32, starting transfers between devices, go(): return lax.ppermute(v, 'dom', perms[name])  28.4 us
    pallas_call x4, Pallas kernels, fetch_turns(): pl.pallas_call(turns_kernel, out_shape=jax.ShapeDtypeStruct((SLOTS, table...  23.6 us
    pallas_call x1, Pallas kernels, by_rows(): pl.pallas_call(table_kernel, out_shape=jax.ShapeDtypeStruct((count, width...  10.2 us
    reduce_sum x4, other arithmetic, drawn(): jnp.sum((negs[:, :, None] == column[None, None, :]).astype(jnp.float32),...  9.31 us
  transfers between devices with their start and end apart: 85, of which 53 were waited for; matrix products, arithmetic and copies ran while one was open for 4% of the time, Pallas kernels for 11%

commit v1 on v0

--- a/solution.py
+++ b/solution.py
@@ -71,10 +71,10 @@
     return [both, r, l, f], early, late
 
 
-def dom_gather(block, early=None):
+def dom_gather(block, early=None, late=None):
     perms = dom_perms()
-    mine, early, _ = spread(block, perms, early)
-    return early, mine + [lax.ppermute(v, "dom", perms["core"]) for v in mine]
+    mine, early, late = spread(block, perms, early, late)
+    return early, late, mine + [lax.ppermute(v, "dom", perms["core"]) for v in mine]
 
 
 def dom_reduce(own, other, early=None, late=None):
@@ -418,11 +418,11 @@
         return fetch_turns(table, arrived[base:base + cap])
 
     arrived, (table,) = tied(arrived, by_rows(relations.T))
-    brought, now_drawn, arrived = spread(held, bucket_perms(), drawn(0), arrived)
-    now_turns = turns(0)
+    brought, _, arrived = spread(held, bucket_perms(), late=arrived)
+    now_turns, now_drawn = turns(0), drawn(0)
     for s in range(steps):
         x, st = select_blocks(brought, roster, s)
-        now_turns, gathered = dom_gather(x, now_turns)
+        now_drawn, now_turns, gathered = dom_gather(x, now_drawn, now_turns)
         own, other = step_grads(s, roster, arrived, now_drawn, gathered, now_turns)
         more = s + 1 < steps
         parts, now_turns, _ = dom_reduce(own, other, turns(s + 1) if more else None)

time: 325 us -> 321 us (0.988)
  waiting for transfers between devices: 132 us -> 108 us
  starting transfers between devices: 87.2 us -> 107 us
    ppermute x32, waiting for transfers between devices: 48.1 us -> 35 us  [go(): return lax.ppermute(v, 'dom', perms[name])]
    ppermute x36, waiting for transfers between devices: 78.4 us -> 67.3 us  [go(): return lax.ppermute(v, perms['axis'], perms[name])]
    ppermute x32, starting transfers between devices: 28.4 us -> 39.4 us  [go(): return lax.ppermute(v, 'dom', perms[name])]
    ppermute x36, starting transfers between devices: 50 us -> 54.1 us  [go(): return lax.ppermute(v, perms['axis'], perms[name])]
    all_to_all x1, starting transfers between devices: 6.79 us -> 10.2 us  [local(): lax.all_to_all(packed, ('bucket', 'dom'), split_axis=0, concat_axis=0, ti...]
  transfers between devices with their start and end apart: 85 -> 85, of which waited for: 53 -> 50; matrix products, arithmetic and copies ran while one was open for 4% -> 4% of each run, Pallas kernels for 11% -> 11%
where the time goes in v1:
time: 321 us; the launch traced here: 315 us
  waiting for transfers between devices  108 us (34%)
  starting transfers between devices  107 us (33%)
  Pallas kernels  77.3 us (24%)
  other arithmetic  11.8 us (4%)
  local copies, waits for them, and re-layouts  9.82 us (3%)
    ppermute x36, waiting for transfers between devices, go(): return lax.ppermute(v, perms['axis'], perms[name])  67.3 us
    ppermute x36, starting transfers between devices, go(): return lax.ppermute(v, perms['axis'], perms[name])  54.1 us
    ppermute x32, starting transfers between devices, go(): return lax.ppermute(v, 'dom', perms[name])  39.4 us
    pallas_call x4, Pallas kernels, step_grads(): pl.pallas_call(functools.partial(step_kernel, step, roster.shape[0]), out...  39.2 us
    ppermute x32, waiting for transfers between devices, go(): return lax.ppermute(v, 'dom', perms[name])  35 us
    pallas_call x4, Pallas kernels, fetch_turns(): pl.pallas_call(turns_kernel, out_shape=jax.ShapeDtypeStruct((SLOTS, table...  23.6 us
    all_to_all x1, starting transfers between devices, local(): lax.all_to_all(packed, ('bucket', 'dom'), split_axis=0, concat_axis=0, ti...  10.2 us
    pallas_call x1, Pallas kernels, by_rows(): pl.pallas_call(table_kernel, out_shape=jax.ShapeDtypeStruct((count, width...  10.2 us
  transfers between devices with their start and end apart: 85, of which 50 were waited for; matrix products, arithmetic and copies ran while one was open for 4% of the time, Pallas kernels for 11%

profile of v1, /device:TPU:6, one launch (start us, length us, event | category | flops | bytes accessed | tf_op | source)
XLA Modules:
  0.0 315.1 jit_solution(6637570559738695960)
XLA Ops:
  6.0 10.2 %all-to-all-start = ((s32[128,1,128]{2,1,0:T(1,128)}), s32[128,1,128]{2,1,0:T(1,128)S(1)}, u32[]{:S(2)}, u32[]{:S(2)}) async-start(s32[128,1,128]{2,1,0:T(1,128)} %copy.64), calls=%async_computation | async-start | bytes 131072 | tf_op jit(solution)/shard_map/all_to_all | solution.py:398
  17.2 3.5 %collective-permute-start.1 = (f32[416,128]{1,0:T(8,128)S(1)}, f32[416,128]{1,0:T(8,128)S(1)}, u32[]{:S(2)}, u32[]{:S(2)}) collective-permute-start(f32[416,128]{1,0:T(8,128)S(1)} %pad_maximum_fusion.refs_0_), channel_id=1, source_target_pairs={{0,64},{16,80},{32,96},{48,112},{64,0},{80,16},{96,32},{112,48},{1... | collective-permute-start | bytes 638984 | tf_op jit(solution)/shard_map/ppermute | solution.py:62
  26.3 10.2 %shard_map.86.table = f32[7424,400]{1,0:T(8,128)} custom-call(f32[400,7424]{1,0:T(8,128)} %bitcast.95), custom_call_target="tpu_custom_call" | custom-call | bytes 27000000 | tf_op jit(solution)/shard_map/pallas_call | solution.py:328
  37.5 3.2 %collective-permute-start.4 = (f32[200,128]{1,0:T(8,128)S(1)}, f32[200,128]{1,0:T(8,128)S(1)}, u32[]{:S(2)}, u32[]{:S(2)}) collective-permute-start(f32[200,128]{1,0:T(8,128)S(1)} %get-tuple-element.74.x_ref), channel_id=1, source_target_pairs={{0,8},{1,9},{2,10},{3,11},{4,12},{5,13},{6,14},{7,15},{8,0},{9,1},... | collective-permute-start | bytes 307208 | tf_op jit(solution)/shard_map/ppermute | solution.py:62
  40.7 3.1 collective-permute-done.4
  45.3 3.2 %collective-permute-start.5 = (f32[400,128]{1,0:T(8,128)S(1)}, f32[400,128]{1,0:T(8,128)S(1)}, u32[]{:S(2)}, u32[]{:S(2)}) collective-permute-start(f32[400,128]{1,0:T(8,128)S(1)} %constant_dynamic-update-slice_fusion.refs_0_), channel_id=1, source_target_pairs={{0,2},{1,3},{2,4},{3,5},{4,6},{5,7},{6,0},{7,1},{8,10},{9,11},{10,... | collective-permute-start | bytes 614408 | tf_op jit(solution)/shard_map/ppermute | solution.py:62
  48.5 5.3 %copy-done = f32[7424,400]{1,0:T(8,128)S(1)} copy-done((f32[7424,400]{1,0:T(8,128)S(1)}, f32[7424,400]{1,0:T(8,128)}, u32[]{:S(2)}) %copy-start) | copy-done | bytes 11878424
  53.9 5.9 %shard_map.88.refs_8_ = f32[1024,400]{1,0:T(8,128)S(1)} custom-call(s32[8,128]{1,0:T(8,128)S(1)} %get-tuple-element.161.ids, f32[7424,400]{1,0:T(8,128)S(1)} %copy-done), custom_call_target="tpu_custom_call" | custom-call | bytes 20000000 | tf_op jit(solution)/shard_map/pallas_call | solution.py:355
  62.2 9.8 %shard_map.89 = (f32[2,200,128]{2,1,0:T(8,128)S(1)}, f32[2,200,128]{2,1,0:T(8,128)S(1)}, f32[4,200,128]{2,1,0:T(8,128)S(1)}, f32[2,200,128]{2,1,0:T(8,128)S(1)},...) custom-call(s32[4,16]{1,0:T(4,128)S(1)} %copy.74.roster, s32[128,128]{1,0:T(8,128)S(1)} %bitcast.91, ...), custom_call_target="tpu_custom_call" | custom-call | flops 6000000000 | bytes 6000000 | tf_op jit(solution)/shard_map/pallas_call | solution.py:368
  75.7 5.9 %shard_map.90.refs_8_ = f32[1024,400]{1,0:T(8,128)S(1)} custom-call(s32[8,128]{1,0:T(8,128)S(1)} %get-tuple-element.160.ids, f32[7424,400]{1,0:T(8,128)S(1)} %bitcast.89), custom_call_target="tpu_custom_call" | custom-call | bytes 20000000 | tf_op jit(solution)/shard_map/pallas_call | solution.py:355
  83.0 3.2 %collective-permute-start.17 = (f32[200,128]{1,0:T(8,128)S(1)}, f32[200,128]{1,0:T(8,128)S(1)}, u32[]{:S(2)}, u32[]{:S(2)}) collective-permute-start(f32[200,128]{1,0:T(8,128)S(1)} %get-tuple-element.86), channel_id=1, source_target_pairs={{0,2},{1,3},{2,4},{3,5},{4,6},{5,7},{6,0},{7,1},{8,10},{9,11},{10,... | collective-permute-start | bytes 307208 | tf_op jit(solution)/shard_map/ppermute | solution.py:84
  86.2 2.6 collective-permute-done.18
  88.8 3.2 %collective-permute-start.19 = (f32[200,128]{1,0:T(8,128)S(1)}, f32[200,128]{1,0:T(8,128)S(1)}, u32[]{:S(2)}, u32[]{:S(2)}) collective-permute-start(f32[200,128]{1,0:T(8,128)S(1)} %fusion.16), channel_id=1, source_target_pairs={{0,8},{1,9},{2,10},{3,11},{4,12},{5,13},{6,14},{7,15},{8,0},{9,1},... | collective-permute-start | bytes 307208 | tf_op jit(solution)/shard_map/ppermute | solution.py:84
  92.0 3.1 collective-permute-done.19.flipped
  100.1 3.6 %collective-permute-start.22 = (f32[416,128]{1,0:T(8,128)S(1)}, f32[416,128]{1,0:T(8,128)S(1)}, u32[]{:S(2)}, u32[]{:S(2)}) collective-permute-start(f32[416,128]{1,0:T(8,128)S(1)} %pad_maximum_fusion.1.refs_0_), channel_id=1, source_target_pairs={{0,96},{16,112},{32,0},{48,16},{64,32},{80,48},{96,64},{112,80},{1... | collective-permute-start | bytes 638984 | tf_op jit(solution)/shard_map/ppermute | solution.py:62
  103.7 5.0 %collective-permute-done.21.refs_1_ = f32[416,128]{1,0:T(8,128)S(1)} collective-permute-done((f32[416,128]{1,0:T(8,128)S(1)}, f32[416,128]{1,0:T(8,128)S(1)}, u32[]{:S(2)}, u32[]{:S(2)}) %collective-permute-start.21) | collective-permute-done | bytes 213024 | tf_op jit(solution)/shard_map/ppermute | solution.py:62
  111.8 3.5 %collective-permute-start.24 = (f32[200,128]{1,0:T(8,128)S(1)}, f32[200,128]{1,0:T(8,128)S(1)}, u32[]{:S(2)}, u32[]{:S(2)}) collective-permute-start(f32[200,128]{1,0:T(8,128)S(1)} %get-tuple-element.90.x_ref), channel_id=1, source_target_pairs={{0,8},{1,9},{2,10},{3,11},{4,12},{5,13},{6,14},{7,15},{8,0},{9,1},... | collective-permute-start | bytes 307208 | tf_op jit(solution)/shard_map/ppermute | solution.py:62
  115.4 2.7 collective-permute-done.24
  120.3 5.3 %collective-permute-done.27.refs_3_ = f32[400,128]{1,0:T(8,128)S(1)} collective-permute-done((f32[400,128]{1,0:T(8,128)S(1)}, f32[400,128]{1,0:T(8,128)S(1)}, u32[]{:S(2)}, u32[]{:S(2)}) %collective-permute-start.27) | collective-permute-done | bytes 204832 | tf_op jit(solution)/shard_map/ppermute | solution.py:62
  129.1 9.8 %shard_map.93 = (f32[2,200,128]{2,1,0:T(8,128)S(1)}, f32[2,200,128]{2,1,0:T(8,128)S(1)}, f32[4,200,128]{2,1,0:T(8,128)S(1)}, f32[2,200,128]{2,1,0:T(8,128)S(1)},...) custom-call(s32[4,16]{1,0:T(4,128)S(1)} %copy.74.roster, s32[128,128]{1,0:T(8,128)S(1)} %bitcast.92, ...), custom_call_target="tpu_custom_call" | custom-call | flops 6000000000 | bytes 6000000 | tf_op jit(solution)/shard_map/pallas_call | solution.py:368
  142.8 5.9 %shard_map.94.refs_8_ = f32[1024,400]{1,0:T(8,128)S(1)} custom-call(s32[8,128]{1,0:T(8,128)S(1)} %get-tuple-element.159.ids, f32[7424,400]{1,0:T(8,128)S(1)} %bitcast.89), custom_call_target="tpu_custom_call" | custom-call | bytes 20000000 | tf_op jit(solution)/shard_map/pallas_call | solution.py:355
  149.8 3.0 collective-permute-start.37
  152.8 2.6 collective-permute-done.38
  155.4 3.6 %collective-permute-start.39 = (f32[200,128]{1,0:T(8,128)S(1)}, f32[200,128]{1,0:T(8,128)S(1)}, u32[]{:S(2)}, u32[]{:S(2)}) collective-permute-start(f32[200,128]{1,0:T(8,128)S(1)} %fusion.11), channel_id=1, source_target_pairs={{0,8},{1,9},{2,10},{3,11},{4,12},{5,13},{6,14},{7,15},{8,0},{9,1},... | collective-permute-start | bytes 307208 | tf_op jit(solution)/shard_map/ppermute | solution.py:84
  159.0 3.1 collective-permute-done.39.flipped
  167.1 3.2 %collective-permute-start.42 = (f32[416,128]{1,0:T(8,128)S(1)}, f32[416,128]{1,0:T(8,128)S(1)}, u32[]{:S(2)}, u32[]{:S(2)}) collective-permute-start(f32[416,128]{1,0:T(8,128)S(1)} %pad_maximum_fusion.2.refs_0_), channel_id=1, source_target_pairs={{0,96},{16,112},{32,0},{48,16},{64,32},{80,48},{96,64},{112,80},{1... | collective-permute-start | bytes 638984 | tf_op jit(solution)/shard_map/ppermute | solution.py:62
  170.5 4.3 %collective-permute-done.41.refs_1_ = f32[416,128]{1,0:T(8,128)S(1)} collective-permute-done((f32[416,128]{1,0:T(8,128)S(1)}, f32[416,128]{1,0:T(8,128)S(1)}, u32[]{:S(2)}, u32[]{:S(2)}) %collective-permute-start.41) | collective-permute-done | bytes 213024 | tf_op jit(solution)/shard_map/ppermute | solution.py:62
  178.4 4.1 %collective-permute-start.44 = (f32[200,128]{1,0:T(8,128)S(1)}, f32[200,128]{1,0:T(8,128)S(1)}, u32[]{:S(2)}, u32[]{:S(2)}) collective-permute-start(f32[200,128]{1,0:T(8,128)S(1)} %get-tuple-element.107.x_ref), channel_id=1, source_target_pairs={{0,8},{1,9},{2,10},{3,11},{4,12},{5,13},{6,14},{7,15},{8,0},{9,1},... | collective-permute-start | bytes 307208 | tf_op jit(solution)/shard_map/ppermute | solution.py:62
  187.3 5.2 %collective-permute-done.47.refs_3_ = f32[400,128]{1,0:T(8,128)S(1)} collective-permute-done((f32[400,128]{1,0:T(8,128)S(1)}, f32[400,128]{1,0:T(8,128)S(1)}, u32[]{:S(2)}, u32[]{:S(2)}) %collective-permute-start.47) | collective-permute-done | bytes 204832 | tf_op jit(solution)/shard_map/ppermute | solution.py:62
  196.3 9.8 %shard_map.97 = (f32[2,200,128]{2,1,0:T(8,128)S(1)}, f32[2,200,128]{2,1,0:T(8,128)S(1)}, f32[4,200,128]{2,1,0:T(8,128)S(1)}, f32[2,200,128]{2,1,0:T(8,128)S(1)},...) custom-call(s32[4,16]{1,0:T(4,128)S(1)} %copy.74.roster, s32[128,128]{1,0:T(8,128)S(1)} %bitcast.93, ...), custom_call_target="tpu_custom_call" | custom-call | flops 6000000000 | bytes 6000000 | tf_op jit(solution)/shard_map/pallas_call | solution.py:368
  209.9 5.9 %shard_map.98.refs_8_ = f32[1024,400]{1,0:T(8,128)S(1)} custom-call(s32[8,128]{1,0:T(8,128)S(1)} %get-tuple-element.158.ids, f32[7424,400]{1,0:T(8,128)S(1)} %bitcast.89), custom_call_target="tpu_custom_call" | custom-call | bytes 20000000 | tf_op jit(solution)/shard_map/pallas_call | solution.py:355
  216.9 3.0 collective-permute-start.57
  219.8 2.6 collective-permute-done.58
  222.5 3.6 %collective-permute-start.59 = (f32[200,128]{1,0:T(8,128)S(1)}, f32[200,128]{1,0:T(8,128)S(1)}, u32[]{:S(2)}, u32[]{:S(2)}) collective-permute-start(f32[200,128]{1,0:T(8,128)S(1)} %fusion.6), channel_id=1, source_target_pairs={{0,8},{1,9},{2,10},{3,11},{4,12},{5,13},{6,14},{7,15},{8,0},{9,1},... | collective-permute-start | bytes 307208 | tf_op jit(solution)/shard_map/ppermute | solution.py:84
  226.1 3.0 collective-permute-done.59.flipped
  234.6 3.1 collective-permute-start.62
  238.0 4.3 %collective-permute-done.61.refs_1_ = f32[416,128]{1,0:T(8,128)S(1)} collective-permute-done((f32[416,128]{1,0:T(8,128)S(1)}, f32[416,128]{1,0:T(8,128)S(1)}, u32[]{:S(2)}, u32[]{:S(2)}) %collective-permute-start.61) | collective-permute-done | bytes 213024 | tf_op jit(solution)/shard_map/ppermute | solution.py:62
  245.8 4.1 %collective-permute-start.64 = (f32[200,128]{1,0:T(8,128)S(1)}, f32[200,128]{1,0:T(8,128)S(1)}, u32[]{:S(2)}, u32[]{:S(2)}) collective-permute-start(f32[200,128]{1,0:T(8,128)S(1)} %get-tuple-element.124.x_ref), channel_id=1, source_target_pairs={{0,8},{1,9},{2,10},{3,11},{4,12},{5,13},{6,14},{7,15},{8,0},{9,1},... | collective-permute-start | bytes 307208 | tf_op jit(solution)/shard_map/ppermute | solution.py:62
  254.7 5.2 %collective-permute-done.67.refs_3_ = f32[400,128]{1,0:T(8,128)S(1)} collective-permute-done((f32[400,128]{1,0:T(8,128)S(1)}, f32[400,128]{1,0:T(8,128)S(1)}, u32[]{:S(2)}, u32[]{:S(2)}) %collective-permute-start.67) | collective-permute-done | bytes 204832 | tf_op jit(solution)/shard_map/ppermute | solution.py:62
  263.5 9.8 %shard_map.101 = (f32[2,200,128]{2,1,0:T(8,128)S(1)}, f32[2,200,128]{2,1,0:T(8,128)S(1)}, f32[4,200,128]{2,1,0:T(8,128)S(1)}, f32[2,200,128]{2,1,0:T(8,128)S(1)}...) custom-call(s32[4,16]{1,0:T(4,128)S(1)} %copy.74.roster, s32[128,128]{1,0:T(8,128)S(1)} %bitcast.94, ...), custom_call_target="tpu_custom_call" | custom-call | flops 6000000000 | bytes 6000000 | tf_op jit(solution)/shard_map/pallas_call | solution.py:368
  277.3 5.0 %collective-permute-done.76 = f32[2,200,128]{2,1,0:T(8,128)S(1)} collective-permute-done((f32[2,200,128]{2,1,0:T(8,128)S(1)}, f32[2,200,128]{2,1,0:T(8,128)S(1)}, u32[]{:S(2)}, u32[]{:S(2)}) %collective-permute-start.76) | collective-permute-done | bytes 204832 | tf_op jit(solution)/shard_map/ppermute | solution.py:84
  284.3 3.0 collective-permute-start.77
  287.3 2.6 collective-permute-done.78
  289.9 3.6 %collective-permute-start.79 = (f32[200,128]{1,0:T(8,128)S(1)}, f32[200,128]{1,0:T(8,128)S(1)}, u32[]{:S(2)}, u32[]{:S(2)}) collective-permute-start(f32[200,128]{1,0:T(8,128)S(1)} %fusion.2), channel_id=1, source_target_pairs={{0,8},{1,9},{2,10},{3,11},{4,12},{5,13},{6,14},{7,15},{8,0},{9,1},... | collective-permute-start | bytes 307208 | tf_op jit(solution)/shard_map/ppermute | solution.py:84
  293.5 3.1 collective-permute-done.79.flipped
  298.0 3.6 %collective-permute-done.80 = f32[208,128]{1,0:T(8,128)S(1)} collective-permute-done((f32[208,128]{1,0:T(8,128)S(1)}, f32[208,128]{1,0:T(8,128)S(1)}, u32[]{:S(2)}, u32[]{:S(2)}) %collective-permute-start.80) | collective-permute-done | bytes 106528 | tf_op jit(solution)/shard_map/ppermute | solution.py:62
  302.1 2.8 collective-permute-start.82
  305.2 4.3 %collective-permute-done.81.refs_1_ = f32[416,128]{1,0:T(8,128)S(1)} collective-permute-done((f32[416,128]{1,0:T(8,128)S(1)}, f32[416,128]{1,0:T(8,128)S(1)}, u32[]{:S(2)}, u32[]{:S(2)}) %collective-permute-start.81) | collective-permute-done | bytes 213024 | tf_op jit(solution)/shard_map/ppermute | solution.py:62
  (206 shorter events, 93.9 us)
Async XLA Ops:
  2.6 14.5 %collective-permute-start = (f32[208,128]{1,0:T(8,128)S(1)}, f32[208,128]{1,0:T(8,128)S(1)}, u32[]{:S(2)}, u32[]{:S(2)}) collective-permute-start(f32[208,128]{1,0:T(8,128)S(1)} %pad_maximum_fusion.5), channel_id=1, source_target_pairs={{0,16},{16,0},{32,48},{48,32},{64,80},{80,64},{96,112},{112,96},{1... | collective-permute-start | bytes 319496 | tf_op jit(solution)/shard_map/ppermute | solution.py:62
  6.0 30.6 %all-to-all-start = ((s32[128,1,128]{2,1,0:T(1,128)}), s32[128,1,128]{2,1,0:T(1,128)S(1)}, u32[]{:S(2)}, u32[]{:S(2)}) async-start(s32[128,1,128]{2,1,0:T(1,128)} %copy.64), calls=%async_computation | async-start | bytes 131072 | tf_op jit(solution)/shard_map/all_to_all | solution.py:398
  17.2 19.5 %collective-permute-start.1 = (f32[416,128]{1,0:T(8,128)S(1)}, f32[416,128]{1,0:T(8,128)S(1)}, u32[]{:S(2)}, u32[]{:S(2)}) collective-permute-start(f32[416,128]{1,0:T(8,128)S(1)} %pad_maximum_fusion.refs_0_), channel_id=1, source_target_pairs={{0,64},{16,80},{32,96},{48,112},{64,0},{80,16},{96,32},{112,48},{1... | collective-permute-start | bytes 638984 | tf_op jit(solution)/shard_map/ppermute | solution.py:62
  20.7 16.0 %collective-permute-start.2 = (f32[416,128]{1,0:T(8,128)S(1)}, f32[416,128]{1,0:T(8,128)S(1)}, u32[]{:S(2)}, u32[]{:S(2)}) collective-permute-start(f32[416,128]{1,0:T(8,128)S(1)} %pad_maximum_fusion.refs_0_), channel_id=1, source_target_pairs={{0,32},{16,48},{32,64},{48,80},{64,96},{80,112},{96,0},{112,16},{1... | collective-permute-start | bytes 638984 | tf_op jit(solution)/shard_map/ppermute | solution.py:62
  21.6 15.2 %collective-permute-start.3 = (f32[416,128]{1,0:T(8,128)S(1)}, f32[416,128]{1,0:T(8,128)S(1)}, u32[]{:S(2)}, u32[]{:S(2)}) collective-permute-start(f32[416,128]{1,0:T(8,128)S(1)} %pad_maximum_fusion.refs_0_), channel_id=1, source_target_pairs={{0,96},{16,112},{32,0},{48,16},{64,32},{80,48},{96,64},{112,80},{1... | collective-permute-start | bytes 638984 | tf_op jit(solution)/shard_map/ppermute | solution.py:62
  43.8 16.1 %collective-permute-start.7 = (f32[400,128]{1,0:T(8,128)S(1)}, f32[400,128]{1,0:T(8,128)S(1)}, u32[]{:S(2)}, u32[]{:S(2)}) collective-permute-start(f32[400,128]{1,0:T(8,128)S(1)} %constant_dynamic-update-slice_fusion.refs_0_), channel_id=1, source_target_pairs={{0,4},{1,5},{2,6},{3,7},{4,0},{5,1},{6,2},{7,3},{8,12},{9,13},{10,... | collective-permute-start | bytes 614408 | tf_op jit(solution)/shard_map/ppermute | solution.py:62
  45.3 15.1 %collective-permute-start.6 = (f32[400,128]{1,0:T(8,128)S(1)}, f32[400,128]{1,0:T(8,128)S(1)}, u32[]{:S(2)}, u32[]{:S(2)}) collective-permute-start(f32[400,128]{1,0:T(8,128)S(1)} %constant_dynamic-update-slice_fusion.refs_0_), channel_id=1, source_target_pairs={{0,6},{1,7},{2,0},{3,1},{4,2},{5,3},{6,4},{7,5},{8,14},{9,15},{10,... | collective-permute-start | bytes 614408 | tf_op jit(solution)/shard_map/ppermute | solution.py:62
  45.3 15.2 %collective-permute-start.5 = (f32[400,128]{1,0:T(8,128)S(1)}, f32[400,128]{1,0:T(8,128)S(1)}, u32[]{:S(2)}, u32[]{:S(2)}) collective-permute-start(f32[400,128]{1,0:T(8,128)S(1)} %constant_dynamic-update-slice_fusion.refs_0_), channel_id=1, source_target_pairs={{0,2},{1,3},{2,4},{3,5},{4,6},{5,7},{6,0},{7,1},{8,10},{9,11},{10,... | collective-permute-start | bytes 614408 | tf_op jit(solution)/shard_map/ppermute | solution.py:62
  72.6 10.3 %collective-permute-start.12 = (f32[4,200,128]{2,1,0:T(8,128)S(1)}, f32[4,200,128]{2,1,0:T(8,128)S(1)}, u32[]{:S(2)}, u32[]{:S(2)}) collective-permute-start(f32[4,200,128]{2,1,0:T(8,128)S(1)} %get-tuple-element.81), channel_id=1, source_target_pairs={{0,1},{1,0},{2,3},{3,2},{4,5},{5,4},{6,7},{7,6},{8,9},{9,8},{10,11... | collective-permute-start | bytes 1228808 | tf_op jit(solution)/shard_map/ppermute | solution.py:84
  73.5 8.1 %collective-permute-start.16 = (f32[2,200,128]{2,1,0:T(8,128)S(1)}, f32[2,200,128]{2,1,0:T(8,128)S(1)}, u32[]{:S(2)}, u32[]{:S(2)}) collective-permute-start(f32[2,200,128]{2,1,0:T(8,128)S(1)} %add.241), channel_id=1, source_target_pairs={{0,2},{1,3},{2,4},{3,5},{4,6},{5,7},{6,0},{7,1},{8,10},{9,11},{10,... | collective-permute-start | bytes 614408 | tf_op jit(solution)/shard_map/ppermute | solution.py:84
  74.5 8.3 %collective-permute-start.14 = (f32[2,200,128]{2,1,0:T(8,128)S(1)}, f32[2,200,128]{2,1,0:T(8,128)S(1)}, u32[]{:S(2)}, u32[]{:S(2)}) collective-permute-start(f32[2,200,128]{2,1,0:T(8,128)S(1)} %add.239), channel_id=1, source_target_pairs={{0,6},{1,7},{2,0},{3,1},{4,2},{5,3},{6,4},{7,5},{8,14},{9,15},{10,... | collective-permute-start | bytes 614408 | tf_op jit(solution)/shard_map/ppermute | solution.py:84
  83.0 9.1 %collective-permute-start.17 = (f32[200,128]{1,0:T(8,128)S(1)}, f32[200,128]{1,0:T(8,128)S(1)}, u32[]{:S(2)}, u32[]{:S(2)}) collective-permute-start(f32[200,128]{1,0:T(8,128)S(1)} %get-tuple-element.86), channel_id=1, source_target_pairs={{0,2},{1,3},{2,4},{3,5},{4,6},{5,7},{6,0},{7,1},{8,10},{9,11},{10,... | collective-permute-start | bytes 307208 | tf_op jit(solution)/shard_map/ppermute | solution.py:84
  100.0 8.7 %collective-permute-start.21 = (f32[416,128]{1,0:T(8,128)S(1)}, f32[416,128]{1,0:T(8,128)S(1)}, u32[]{:S(2)}, u32[]{:S(2)}) collective-permute-start(f32[416,128]{1,0:T(8,128)S(1)} %pad_maximum_fusion.1.refs_0_), channel_id=1, source_target_pairs={{0,32},{16,48},{32,64},{48,80},{64,96},{80,112},{96,0},{112,16},{1... | collective-permute-start | bytes 638984 | tf_op jit(solution)/shard_map/ppermute | solution.py:62
  100.1 9.3 %collective-permute-start.22 = (f32[416,128]{1,0:T(8,128)S(1)}, f32[416,128]{1,0:T(8,128)S(1)}, u32[]{:S(2)}, u32[]{:S(2)}) collective-permute-start(f32[416,128]{1,0:T(8,128)S(1)} %pad_maximum_fusion.1.refs_0_), channel_id=1, source_target_pairs={{0,96},{16,112},{32,0},{48,16},{64,32},{80,48},{96,64},{112,80},{1... | collective-permute-start | bytes 638984 | tf_op jit(solution)/shard_map/ppermute | solution.py:62
  103.7 7.3 %collective-permute-start.23 = (f32[416,128]{1,0:T(8,128)S(1)}, f32[416,128]{1,0:T(8,128)S(1)}, u32[]{:S(2)}, u32[]{:S(2)}) collective-permute-start(f32[416,128]{1,0:T(8,128)S(1)} %pad_maximum_fusion.1.refs_0_), channel_id=1, source_target_pairs={{0,64},{16,80},{32,96},{48,112},{64,0},{80,16},{96,32},{112,48},{1... | collective-permute-start | bytes 638984 | tf_op jit(solution)/shard_map/ppermute | solution.py:62
  118.1 7.4 %collective-permute-start.27 = (f32[400,128]{1,0:T(8,128)S(1)}, f32[400,128]{1,0:T(8,128)S(1)}, u32[]{:S(2)}, u32[]{:S(2)}) collective-permute-start(f32[400,128]{1,0:T(8,128)S(1)} %constant_dynamic-update-slice_fusion.2.refs_0_), channel_id=1, source_target_pairs={{0,4},{1,5},{2,6},{3,7},{4,0},{5,1},{6,2},{7,3},{8,12},{9,13},{10,... | collective-permute-start | bytes 614408 | tf_op jit(solution)/shard_map/ppermute | solution.py:62
  118.2 7.4 %collective-permute-start.25 = (f32[400,128]{1,0:T(8,128)S(1)}, f32[400,128]{1,0:T(8,128)S(1)}, u32[]{:S(2)}, u32[]{:S(2)}) collective-permute-start(f32[400,128]{1,0:T(8,128)S(1)} %constant_dynamic-update-slice_fusion.2.refs_0_), channel_id=1, source_target_pairs={{0,2},{1,3},{2,4},{3,5},{4,6},{5,7},{6,0},{7,1},{8,10},{9,11},{10,... | collective-permute-start | bytes 614408 | tf_op jit(solution)/shard_map/ppermute | solution.py:62
  119.6 8.0 %collective-permute-start.26 = (f32[400,128]{1,0:T(8,128)S(1)}, f32[400,128]{1,0:T(8,128)S(1)}, u32[]{:S(2)}, u32[]{:S(2)}) collective-permute-start(f32[400,128]{1,0:T(8,128)S(1)} %constant_dynamic-update-slice_fusion.2.refs_0_), channel_id=1, source_target_pairs={{0,6},{1,7},{2,0},{3,1},{4,2},{5,3},{6,4},{7,5},{8,14},{9,15},{10,... | collective-permute-start | bytes 614408 | tf_op jit(solution)/shard_map/ppermute | solution.py:62
  120.3 7.4 %collective-permute-start.28 = (f32[400,128]{1,0:T(8,128)S(1)}, f32[400,128]{1,0:T(8,128)S(1)}, u32[]{:S(2)}, u32[]{:S(2)}) collective-permute-start(f32[400,128]{1,0:T(8,128)S(1)} %constant_dynamic-update-slice_fusion.2.refs_0_), channel_id=1, source_target_pairs={{0,1},{1,0},{2,3},{3,2},{4,5},{5,4},{6,7},{7,6},{8,9},{9,8},{10,11... | collective-permute-start | bytes 614408 | tf_op jit(solution)/shard_map/ppermute | solution.py:77
  139.5 9.9 %collective-permute-start.32 = (f32[4,200,128]{2,1,0:T(8,128)S(1)}, f32[4,200,128]{2,1,0:T(8,128)S(1)}, u32[]{:S(2)}, u32[]{:S(2)}) collective-permute-start(f32[4,200,128]{2,1,0:T(8,128)S(1)} %get-tuple-element.98), channel_id=1, source_target_pairs={{0,1},{1,0},{2,3},{3,2},{4,5},{5,4},{6,7},{7,6},{8,9},{9,8},{10,11... | collective-permute-start | bytes 1228808 | tf_op jit(solution)/shard_map/ppermute | solution.py:84
  140.5 8.3 %collective-permute-start.36 = (f32[2,200,128]{2,1,0:T(8,128)S(1)}, f32[2,200,128]{2,1,0:T(8,128)S(1)}, u32[]{:S(2)}, u32[]{:S(2)}) collective-permute-start(f32[2,200,128]{2,1,0:T(8,128)S(1)} %add.256), channel_id=1, source_target_pairs={{0,2},{1,3},{2,4},{3,5},{4,6},{5,7},{6,0},{7,1},{8,10},{9,11},{10,... | collective-permute-start | bytes 614408 | tf_op jit(solution)/shard_map/ppermute | solution.py:84
  141.1 8.3 %collective-permute-start.34 = (f32[2,200,128]{2,1,0:T(8,128)S(1)}, f32[2,200,128]{2,1,0:T(8,128)S(1)}, u32[]{:S(2)}, u32[]{:S(2)}) collective-permute-start(f32[2,200,128]{2,1,0:T(8,128)S(1)} %add.254), channel_id=1, source_target_pairs={{0,6},{1,7},{2,0},{3,1},{4,2},{5,3},{6,4},{7,5},{8,14},{9,15},{10,... | collective-permute-start | bytes 614408 | tf_op jit(solution)/shard_map/ppermute | solution.py:84
  149.8 9.2 %collective-permute-start.37 = (f32[200,128]{1,0:T(8,128)S(1)}, f32[200,128]{1,0:T(8,128)S(1)}, u32[]{:S(2)}, u32[]{:S(2)}) collective-permute-start(f32[200,128]{1,0:T(8,128)S(1)} %get-tuple-element.103), channel_id=1, source_target_pairs={{0,2},{1,3},{2,4},{3,5},{4,6},{5,7},{6,0},{7,1},{8,10},{9,11},{10,... | collective-permute-start | bytes 307208 | tf_op jit(solution)/shard_map/ppermute | solution.py:84
  167.0 7.8 %collective-permute-start.41 = (f32[416,128]{1,0:T(8,128)S(1)}, f32[416,128]{1,0:T(8,128)S(1)}, u32[]{:S(2)}, u32[]{:S(2)}) collective-permute-start(f32[416,128]{1,0:T(8,128)S(1)} %pad_maximum_fusion.2.refs_0_), channel_id=1, source_target_pairs={{0,32},{16,48},{32,64},{48,80},{64,96},{80,112},{96,0},{112,16},{1... | collective-permute-start | bytes 638984 | tf_op jit(solution)/shard_map/ppermute | solution.py:62
  167.1 8.9 %collective-permute-start.42 = (f32[416,128]{1,0:T(8,128)S(1)}, f32[416,128]{1,0:T(8,128)S(1)}, u32[]{:S(2)}, u32[]{:S(2)}) collective-permute-start(f32[416,128]{1,0:T(8,128)S(1)} %pad_maximum_fusion.2.refs_0_), channel_id=1, source_target_pairs={{0,96},{16,112},{32,0},{48,16},{64,32},{80,48},{96,64},{112,80},{1... | collective-permute-start | bytes 638984 | tf_op jit(solution)/shard_map/ppermute | solution.py:62
  170.3 7.3 %collective-permute-start.43 = (f32[416,128]{1,0:T(8,128)S(1)}, f32[416,128]{1,0:T(8,128)S(1)}, u32[]{:S(2)}, u32[]{:S(2)}) collective-permute-start(f32[416,128]{1,0:T(8,128)S(1)} %pad_maximum_fusion.2.refs_0_), channel_id=1, source_target_pairs={{0,64},{16,80},{32,96},{48,112},{64,0},{80,16},{96,32},{112,48},{1... | collective-permute-start | bytes 638984 | tf_op jit(solution)/shard_map/ppermute | solution.py:62
  185.1 7.4 %collective-permute-start.47 = (f32[400,128]{1,0:T(8,128)S(1)}, f32[400,128]{1,0:T(8,128)S(1)}, u32[]{:S(2)}, u32[]{:S(2)}) collective-permute-start(f32[400,128]{1,0:T(8,128)S(1)} %constant_dynamic-update-slice_fusion.4.refs_0_), channel_id=1, source_target_pairs={{0,4},{1,5},{2,6},{3,7},{4,0},{5,1},{6,2},{7,3},{8,12},{9,13},{10,... | collective-permute-start | bytes 614408 | tf_op jit(solution)/shard_map/ppermute | solution.py:62
  185.2 7.3 %collective-permute-start.45 = (f32[400,128]{1,0:T(8,128)S(1)}, f32[400,128]{1,0:T(8,128)S(1)}, u32[]{:S(2)}, u32[]{:S(2)}) collective-permute-start(f32[400,128]{1,0:T(8,128)S(1)} %constant_dynamic-update-slice_fusion.4.refs_0_), channel_id=1, source_target_pairs={{0,2},{1,3},{2,4},{3,5},{4,6},{5,7},{6,0},{7,1},{8,10},{9,11},{10,... | collective-permute-start | bytes 614408 | tf_op jit(solution)/shard_map/ppermute | solution.py:62
  186.9 7.8 %collective-permute-start.46 = (f32[400,128]{1,0:T(8,128)S(1)}, f32[400,128]{1,0:T(8,128)S(1)}, u32[]{:S(2)}, u32[]{:S(2)}) collective-permute-start(f32[400,128]{1,0:T(8,128)S(1)} %constant_dynamic-update-slice_fusion.4.refs_0_), channel_id=1, source_target_pairs={{0,6},{1,7},{2,0},{3,1},{4,2},{5,3},{6,4},{7,5},{8,14},{9,15},{10,... | collective-permute-start | bytes 614408 | tf_op jit(solution)/shard_map/ppermute | solution.py:62
  187.3 7.6 %collective-permute-start.48 = (f32[400,128]{1,0:T(8,128)S(1)}, f32[400,128]{1,0:T(8,128)S(1)}, u32[]{:S(2)}, u32[]{:S(2)}) collective-permute-start(f32[400,128]{1,0:T(8,128)S(1)} %constant_dynamic-update-slice_fusion.4.refs_0_), channel_id=1, source_target_pairs={{0,1},{1,0},{2,3},{3,2},{4,5},{5,4},{6,7},{7,6},{8,9},{9,8},{10,11... | collective-permute-start | bytes 614408 | tf_op jit(solution)/shard_map/ppermute | solution.py:77
  206.7 9.7 %collective-permute-start.52 = (f32[4,200,128]{2,1,0:T(8,128)S(1)}, f32[4,200,128]{2,1,0:T(8,128)S(1)}, u32[]{:S(2)}, u32[]{:S(2)}) collective-permute-start(f32[4,200,128]{2,1,0:T(8,128)S(1)} %get-tuple-element.115), channel_id=1, source_target_pairs={{0,1},{1,0},{2,3},{3,2},{4,5},{5,4},{6,7},{7,6},{8,9},{9,8},{10,11... | collective-permute-start | bytes 1228808 | tf_op jit(solution)/shard_map/ppermute | solution.py:84
  207.7 8.1 %collective-permute-start.56 = (f32[2,200,128]{2,1,0:T(8,128)S(1)}, f32[2,200,128]{2,1,0:T(8,128)S(1)}, u32[]{:S(2)}, u32[]{:S(2)}) collective-permute-start(f32[2,200,128]{2,1,0:T(8,128)S(1)} %add.271), channel_id=1, source_target_pairs={{0,2},{1,3},{2,4},{3,5},{4,6},{5,7},{6,0},{7,1},{8,10},{9,11},{10,... | collective-permute-start | bytes 614408 | tf_op jit(solution)/shard_map/ppermute | solution.py:84
  208.4 8.1 %collective-permute-start.54 = (f32[2,200,128]{2,1,0:T(8,128)S(1)}, f32[2,200,128]{2,1,0:T(8,128)S(1)}, u32[]{:S(2)}, u32[]{:S(2)}) collective-permute-start(f32[2,200,128]{2,1,0:T(8,128)S(1)} %add.269), channel_id=1, source_target_pairs={{0,6},{1,7},{2,0},{3,1},{4,2},{5,3},{6,4},{7,5},{8,14},{9,15},{10,... | collective-permute-start | bytes 614408 | tf_op jit(solution)/shard_map/ppermute | solution.py:84
  216.9 9.3 %collective-permute-start.57 = (f32[200,128]{1,0:T(8,128)S(1)}, f32[200,128]{1,0:T(8,128)S(1)}, u32[]{:S(2)}, u32[]{:S(2)}) collective-permute-start(f32[200,128]{1,0:T(8,128)S(1)} %get-tuple-element.120), channel_id=1, source_target_pairs={{0,2},{1,3},{2,4},{3,5},{4,6},{5,7},{6,0},{7,1},{8,10},{9,11},{10,... | collective-permute-start | bytes 307208 | tf_op jit(solution)/shard_map/ppermute | solution.py:84
  234.1 8.1 %collective-permute-start.61 = (f32[416,128]{1,0:T(8,128)S(1)}, f32[416,128]{1,0:T(8,128)S(1)}, u32[]{:S(2)}, u32[]{:S(2)}) collective-permute-start(f32[416,128]{1,0:T(8,128)S(1)} %pad_maximum_fusion.3.refs_0_), channel_id=1, source_target_pairs={{0,32},{16,48},{32,64},{48,80},{64,96},{80,112},{96,0},{112,16},{1... | collective-permute-start | bytes 638984 | tf_op jit(solution)/shard_map/ppermute | solution.py:62
  234.6 8.8 %collective-permute-start.62 = (f32[416,128]{1,0:T(8,128)S(1)}, f32[416,128]{1,0:T(8,128)S(1)}, u32[]{:S(2)}, u32[]{:S(2)}) collective-permute-start(f32[416,128]{1,0:T(8,128)S(1)} %pad_maximum_fusion.3.refs_0_), channel_id=1, source_target_pairs={{0,96},{16,112},{32,0},{48,16},{64,32},{80,48},{96,64},{112,80},{1... | collective-permute-start | bytes 638984 | tf_op jit(solution)/shard_map/ppermute | solution.py:62
  237.7 7.3 %collective-permute-start.63 = (f32[416,128]{1,0:T(8,128)S(1)}, f32[416,128]{1,0:T(8,128)S(1)}, u32[]{:S(2)}, u32[]{:S(2)}) collective-permute-start(f32[416,128]{1,0:T(8,128)S(1)} %pad_maximum_fusion.3.refs_0_), channel_id=1, source_target_pairs={{0,64},{16,80},{32,96},{48,112},{64,0},{80,16},{96,32},{112,48},{1... | collective-permute-start | bytes 638984 | tf_op jit(solution)/shard_map/ppermute | solution.py:62
  252.5 7.4 %collective-permute-start.67 = (f32[400,128]{1,0:T(8,128)S(1)}, f32[400,128]{1,0:T(8,128)S(1)}, u32[]{:S(2)}, u32[]{:S(2)}) collective-permute-start(f32[400,128]{1,0:T(8,128)S(1)} %constant_dynamic-update-slice_fusion.6.refs_0_), channel_id=1, source_target_pairs={{0,4},{1,5},{2,6},{3,7},{4,0},{5,1},{6,2},{7,3},{8,12},{9,13},{10,... | collective-permute-start | bytes 614408 | tf_op jit(solution)/shard_map/ppermute | solution.py:62
  252.6 7.3 %collective-permute-start.65 = (f32[400,128]{1,0:T(8,128)S(1)}, f32[400,128]{1,0:T(8,128)S(1)}, u32[]{:S(2)}, u32[]{:S(2)}) collective-permute-start(f32[400,128]{1,0:T(8,128)S(1)} %constant_dynamic-update-slice_fusion.6.refs_0_), channel_id=1, source_target_pairs={{0,2},{1,3},{2,4},{3,5},{4,6},{5,7},{6,0},{7,1},{8,10},{9,11},{10,... | collective-permute-start | bytes 614408 | tf_op jit(solution)/shard_map/ppermute | solution.py:62
  254.3 7.7 %collective-permute-start.66 = (f32[400,128]{1,0:T(8,128)S(1)}, f32[400,128]{1,0:T(8,128)S(1)}, u32[]{:S(2)}, u32[]{:S(2)}) collective-permute-start(f32[400,128]{1,0:T(8,128)S(1)} %constant_dynamic-update-slice_fusion.6.refs_0_), channel_id=1, source_target_pairs={{0,6},{1,7},{2,0},{3,1},{4,2},{5,3},{6,4},{7,5},{8,14},{9,15},{10,... | collective-permute-start | bytes 614408 | tf_op jit(solution)/shard_map/ppermute | solution.py:62
  254.7 7.4 %collective-permute-start.68 = (f32[400,128]{1,0:T(8,128)S(1)}, f32[400,128]{1,0:T(8,128)S(1)}, u32[]{:S(2)}, u32[]{:S(2)}) collective-permute-start(f32[400,128]{1,0:T(8,128)S(1)} %constant_dynamic-update-slice_fusion.6.refs_0_), channel_id=1, source_target_pairs={{0,1},{1,0},{2,3},{3,2},{4,5},{5,4},{6,7},{7,6},{8,9},{9,8},{10,11... | collective-permute-start | bytes 614408 | tf_op jit(solution)/shard_map/ppermute | solution.py:77
  273.9 10.0 %collective-permute-start.72 = (f32[4,200,128]{2,1,0:T(8,128)S(1)}, f32[4,200,128]{2,1,0:T(8,128)S(1)}, u32[]{:S(2)}, u32[]{:S(2)}) collective-permute-start(f32[4,200,128]{2,1,0:T(8,128)S(1)} %get-tuple-element.132), channel_id=1, source_target_pairs={{0,1},{1,0},{2,3},{3,2},{4,5},{5,4},{6,7},{7,6},{8,9},{9,8},{10,11... | collective-permute-start | bytes 1228808 | tf_op jit(solution)/shard_map/ppermute | solution.py:84
  274.8 7.5 %collective-permute-start.76 = (f32[2,200,128]{2,1,0:T(8,128)S(1)}, f32[2,200,128]{2,1,0:T(8,128)S(1)}, u32[]{:S(2)}, u32[]{:S(2)}) collective-permute-start(f32[2,200,128]{2,1,0:T(8,128)S(1)} %add.286), channel_id=1, source_target_pairs={{0,2},{1,3},{2,4},{3,5},{4,6},{5,7},{6,0},{7,1},{8,10},{9,11},{10,... | collective-permute-start | bytes 614408 | tf_op jit(solution)/shard_map/ppermute | solution.py:84
  275.8 8.1 %collective-permute-start.74 = (f32[2,200,128]{2,1,0:T(8,128)S(1)}, f32[2,200,128]{2,1,0:T(8,128)S(1)}, u32[]{:S(2)}, u32[]{:S(2)}) collective-permute-start(f32[2,200,128]{2,1,0:T(8,128)S(1)} %add.284), channel_id=1, source_target_pairs={{0,6},{1,7},{2,0},{3,1},{4,2},{5,3},{6,4},{7,5},{8,14},{9,15},{10,... | collective-permute-start | bytes 614408 | tf_op jit(solution)/shard_map/ppermute | solution.py:84
  284.3 9.3 %collective-permute-start.77 = (f32[200,128]{1,0:T(8,128)S(1)}, f32[200,128]{1,0:T(8,128)S(1)}, u32[]{:S(2)}, u32[]{:S(2)}) collective-permute-start(f32[200,128]{1,0:T(8,128)S(1)} %get-tuple-element.143), channel_id=1, source_target_pairs={{0,2},{1,3},{2,4},{3,5},{4,6},{5,7},{6,0},{7,1},{8,10},{9,11},{10,... | collective-permute-start | bytes 307208 | tf_op jit(solution)/shard_map/ppermute | solution.py:84
  301.6 7.8 %collective-permute-start.81 = (f32[416,128]{1,0:T(8,128)S(1)}, f32[416,128]{1,0:T(8,128)S(1)}, u32[]{:S(2)}, u32[]{:S(2)}) collective-permute-start(f32[416,128]{1,0:T(8,128)S(1)} %pad_maximum_fusion.4.refs_0_), channel_id=1, source_target_pairs={{0,32},{16,48},{32,64},{48,80},{64,96},{80,112},{96,0},{112,16},{1... | collective-permute-start | bytes 638984 | tf_op jit(solution)/shard_map/ppermute | solution.py:62
  302.1 8.5 %collective-permute-start.82 = (f32[416,128]{1,0:T(8,128)S(1)}, f32[416,128]{1,0:T(8,128)S(1)}, u32[]{:S(2)}, u32[]{:S(2)}) collective-permute-start(f32[416,128]{1,0:T(8,128)S(1)} %pad_maximum_fusion.4.refs_0_), channel_id=1, source_target_pairs={{0,96},{16,112},{32,0},{48,16},{64,32},{80,48},{96,64},{112,80},{1... | collective-permute-start | bytes 638984 | tf_op jit(solution)/shard_map/ppermute | solution.py:62
  304.9 7.3 %collective-permute-start.83 = (f32[416,128]{1,0:T(8,128)S(1)}, f32[416,128]{1,0:T(8,128)S(1)}, u32[]{:S(2)}, u32[]{:S(2)}) collective-permute-start(f32[416,128]{1,0:T(8,128)S(1)} %pad_maximum_fusion.4.refs_0_), channel_id=1, source_target_pairs={{0,64},{16,80},{32,96},{48,112},{64,0},{80,16},{96,32},{112,48},{1... | collective-permute-start | bytes 638984 | tf_op jit(solution)/shard_map/ppermute | solution.py:62
  (43 other events, 250.4 us)

commit v2 on v1

--- a/solution.py
+++ b/solution.py
@@ -84,20 +84,17 @@
         return lax.ppermute(v, "dom", perms[name])
 
     swapped = [go(v, "core") for v in other]
-    to_plus, to_minus = own[0] + swapped[0], own[1] + swapped[1]
-    plus, minus = go(to_plus, "plus"), go(to_minus, "minus")
-    on_plus = own[2][0] + swapped[2][0] + plus[0]
-    on_minus = own[2][1] + swapped[2][1] + minus[0]
+    sums = [v + w for v, w in zip(own[1:], swapped[1:])]
+    came = [go(v, name) for v, name in zip(sums, ("far", "plus", "minus"))]
     if early is not None:
-        on_plus, (on_minus, early) = tied(on_plus, on_minus, early)
-    u4, u3 = go(on_plus, "plus"), go(on_minus, "minus")
-    flipped = (own[2][2] + swapped[2][2]) + (plus[1] + u3)
+        came[2], (early,) = tied(came[2], early)
+    flipped = (own[0][1] + swapped[0][1]) + ((came[0][1] + came[1][1]) + came[2][1])
     if late is not None:
         flipped, (late,) = tied(flipped, late)
-    return (own[2], swapped[2], minus, u4, go(flipped, "flip")), early, late
-
-
-OUT_PLACE = {6: (0, 0), 5: (0, 1), 7: (1, 0), 2: (1, 1), 4: (2, 0), 3: (2, 1), 1: (2, 2), 0: (2, 3)}
+    return (own[0], swapped[0], *came, go(flipped, "flip")), early, late
+
+
+OUT_PLACE = {0: (0, 0), 1: (0, 1), 6: (1, 0), 7: (1, 1), 4: (2, 0), 5: (2, 1), 2: (3, 0), 3: (3, 1)}
 
 
 def ring_place(ring):
@@ -163,8 +160,8 @@
     )(roster, *blocks)
 
 
-def adagrad_kernel(own, swapped, minus, ring, flipped, x_ref, st_ref, out_ref):
-    grad = (own[3] + swapped[3]) + ((minus[1] + ring[...]) + flipped[...])
+def adagrad_kernel(own, swapped, far, plus, minus, flipped, x_ref, st_ref, out_ref):
+    grad = (own[0] + swapped[0]) + ((far[0] + plus[0]) + (minus[0] + flipped[...]))
     total = jnp.sum(grad * grad, axis=0, keepdims=True)
     total = jnp.broadcast_to(total, (8, LANES))
     total = total + pltpu.roll(total, 64, 1)
@@ -178,7 +175,7 @@
     return pl.pallas_call(
         adagrad_kernel,
         out_shape=jax.ShapeDtypeStruct((HALF + 8, LANES), jnp.float32),
-        in_specs=[VMEM] * 7,
+        in_specs=[VMEM] * 8,
         out_specs=VMEM,
         compiler_params=pltpu.CompilerParams(vmem_limit_bytes=4 * MIB),
         cost_estimate=pl.CostEstimate(flops=200000, bytes_accessed=700000, transcendentals=0),
@@ -218,7 +215,7 @@
 
 
 def step_kernel(step, steps, roster, arrived, drawn, *refs):
-    arrays, rel, outs, scratch = refs[:-15], refs[-15], refs[-14:-8], refs[-8:]
+    arrays, rel, outs, scratch = refs[:-17], refs[-17], refs[-16:-8], refs[-8:]
     blocks = views(arrays, HALF)
     src, dst, sh, sl, dh, dl, th, tl = scratch
     me = lax.axis_index("bucket")
@@ -283,7 +280,7 @@
         for g, tile in enumerate(tiles):
             p = 4 * t + g
             array, place = OUT_PLACE[p % 8]
-            outs[array + 3 * (p // 8)][place] = tile
+            outs[array + 4 * (p // 8)][place] = tile
 
 
 def table_kernel(columns, out_ref, came, goes, came_sems, goes_sems):
@@ -364,12 +361,12 @@
 
 def step_grads(step, roster, arrived, drawn, blocks, turns):
     f32, bf16 = jnp.float32, jnp.bfloat16
-    shapes = tuple(jax.ShapeDtypeStruct((n, HALF, LANES), f32) for n in (2, 2, 4))
+    shapes = tuple(jax.ShapeDtypeStruct((n, HALF, LANES), f32) for n in (2, 2, 2, 2))
     outs = pl.pallas_call(
         functools.partial(step_kernel, step, roster.shape[0]),
         out_shape=shapes * 2,
         in_specs=[SMEM] + [VMEM] * (3 + len(blocks)),
-        out_specs=(VMEM,) * 6,
+        out_specs=(VMEM,) * 8,
         scratch_shapes=[
             pltpu.VMEM((2 * HALF, PROWS), f32),
             pltpu.VMEM((2 * HALF, PROWS), f32),
@@ -383,7 +380,7 @@
         compiler_params=pltpu.CompilerParams(vmem_limit_bytes=20 * MIB),
         cost_estimate=pl.CostEstimate(flops=6_000_000_000, bytes_accessed=6_000_000, transcendentals=600_000),
     )(roster, arrived, drawn, *blocks, turns)
-    return outs[:3], outs[3:]
+    return outs[:4], outs[4:]
 
 
 def local(entity_table, adagrad_state, relations, roster, edge_triples, counts, negatives):

time: 321 us -> 317 us (0.988)
  the two profiles are of different devices: /device:TPU:6 before, /device:TPU:24 now
where the time goes in v2:
time: 317 us; the launch traced here: 312 us
  waiting for transfers between devices  126 us (40%)
  starting transfers between devices  85.6 us (27%)
  Pallas kernels  77.3 us (24%)
  other arithmetic  11.9 us (4%)
  local copies, waits for them, and re-layouts  9.82 us (3%)
    ppermute x36, waiting for transfers between devices, go(): return lax.ppermute(v, perms['axis'], perms[name])  74.1 us
    ppermute x36, starting transfers between devices, go(): return lax.ppermute(v, perms['axis'], perms[name])  47.8 us
    ppermute x32, waiting for transfers between devices, go(): return lax.ppermute(v, 'dom', perms[name])  46.8 us
    pallas_call x4, Pallas kernels, step_grads(): pl.pallas_call(functools.partial(step_kernel, step, roster.shape[0]), out...  39.2 us
    ppermute x32, starting transfers between devices, go(): return lax.ppermute(v, 'dom', perms[name])  24 us
    pallas_call x4, Pallas kernels, fetch_turns(): pl.pallas_call(turns_kernel, out_shape=jax.ShapeDtypeStruct((SLOTS, table...  23.6 us
    all_to_all x1, starting transfers between devices, local(): lax.all_to_all(packed, ('bucket', 'dom'), split_axis=0, concat_axis=0, ti...  10.8 us
    pallas_call x1, Pallas kernels, by_rows(): pl.pallas_call(table_kernel, out_shape=jax.ShapeDtypeStruct((count, width...  10.1 us
  transfers between devices with their start and end apart: 85, of which 48 were waited for; matrix products, arithmetic and copies ran while one was open for 4% of the time, Pallas kernels for 11%

profile of v2, /device:TPU:24, one launch (start us, length us, event | category | flops | bytes accessed | tf_op | source)
XLA Modules:
  0.0 311.6 jit_solution(14763779846465045880)
XLA Ops:
  5.2 10.8 %all-to-all-start = ((s32[128,1,128]{2,1,0:T(1,128)}), s32[128,1,128]{2,1,0:T(1,128)S(1)}, u32[]{:S(2)}, u32[]{:S(2)}) async-start(s32[128,1,128]{2,1,0:T(1,128)} %copy.64), calls=%async_computation | async-start | bytes 131072 | tf_op jit(solution)/shard_map/all_to_all | solution.py:395
  17.0 3.6 %collective-permute-start.1 = (f32[416,128]{1,0:T(8,128)S(1)}, f32[416,128]{1,0:T(8,128)S(1)}, u32[]{:S(2)}, u32[]{:S(2)}) collective-permute-start(f32[416,128]{1,0:T(8,128)S(1)} %pad_maximum_fusion.refs_0_), channel_id=1, source_target_pairs={{0,64},{16,80},{32,96},{48,112},{64,0},{80,16},{96,32},{112,48},{1... | collective-permute-start | bytes 638984 | tf_op jit(solution)/shard_map/ppermute | solution.py:62
  21.4 2.4 collective-permute-start.3
  23.9 2.3 convert_reduce_fusion.3.drawn
  26.2 10.1 %shard_map.86.table = f32[7424,400]{1,0:T(8,128)} custom-call(f32[400,7424]{1,0:T(8,128)} %bitcast.47), custom_call_target="tpu_custom_call" | custom-call | bytes 27000000 | tf_op jit(solution)/shard_map/pallas_call | solution.py:325
  38.8 4.8 %collective-permute-done.4 = f32[200,128]{1,0:T(8,128)S(1)} collective-permute-done((f32[200,128]{1,0:T(8,128)S(1)}, f32[200,128]{1,0:T(8,128)S(1)}, u32[]{:S(2)}, u32[]{:S(2)}) %collective-permute-start.4) | collective-permute-done | bytes 102432 | tf_op jit(solution)/shard_map/ppermute | solution.py:62
  43.7 3.1 collective-permute-start.7
  48.8 5.3 %copy-done = f32[7424,400]{1,0:T(8,128)S(1)} copy-done((f32[7424,400]{1,0:T(8,128)S(1)}, f32[7424,400]{1,0:T(8,128)}, u32[]{:S(2)}) %copy-start) | copy-done | bytes 11878424
  54.1 5.9 %shard_map.88.refs_8_ = f32[1024,400]{1,0:T(8,128)S(1)} custom-call(s32[8,128]{1,0:T(8,128)S(1)} %get-tuple-element.163.ids, f32[7424,400]{1,0:T(8,128)S(1)} %copy-done), custom_call_target="tpu_custom_call" | custom-call | bytes 20000000 | tf_op jit(solution)/shard_map/pallas_call | solution.py:352
  62.4 9.8 %shard_map.89 = (f32[2,200,128]{2,1,0:T(8,128)S(1)}, f32[2,200,128]{2,1,0:T(8,128)S(1)}, f32[2,200,128]{2,1,0:T(8,128)S(1)}, f32[2,200,128]{2,1,0:T(8,128)S(1)},...) custom-call(s32[4,16]{1,0:T(4,128)S(1)} %copy.74.roster, ...), custom_call_target="tpu_custom_call" | custom-call | flops 6000000000 | bytes 6000000 | tf_op jit(solution)/shard_map/pallas_call | solution.py:365
  73.8 2.4 collective-permute-start.18
  78.1 5.9 %shard_map.90.refs_8_ = f32[1024,400]{1,0:T(8,128)S(1)} custom-call(s32[8,128]{1,0:T(8,128)S(1)} %get-tuple-element.162.ids, f32[7424,400]{1,0:T(8,128)S(1)} %bitcast.41), custom_call_target="tpu_custom_call" | custom-call | bytes 20000000 | tf_op jit(solution)/shard_map/pallas_call | solution.py:352
  85.5 3.5 %collective-permute-done.16.plus = f32[2,200,128]{2,1,0:T(8,128)S(1)} collective-permute-done((f32[2,200,128]{2,1,0:T(8,128)S(1)}, f32[2,200,128]{2,1,0:T(8,128)S(1)}, u32[]{:S(2)}, u32[]{:S(2)}) %collective-permute-start.16) | collective-permute-done | bytes 204832 | tf_op jit(solution)/shard_map/ppermute | solution.py:84
  90.4 4.8 %collective-permute-done.19.flipped = f32[200,128]{1,0:T(8,128)S(1)} collective-permute-done((f32[200,128]{1,0:T(8,128)S(1)}, f32[200,128]{1,0:T(8,128)S(1)}, u32[]{:S(2)}, u32[]{:S(2)}) %collective-permute-start.19) | collective-permute-done | bytes 102432 | tf_op jit(solution)/shard_map/ppermute | solution.py:84
  96.2 2.3 convert_reduce_fusion.2.drawn
  100.3 3.2 %collective-permute-start.22 = (f32[416,128]{1,0:T(8,128)S(1)}, f32[416,128]{1,0:T(8,128)S(1)}, u32[]{:S(2)}, u32[]{:S(2)}) collective-permute-start(f32[416,128]{1,0:T(8,128)S(1)} %pad_maximum_fusion.1.refs_0_), channel_id=1, source_target_pairs={{0,96},{16,112},{32,0},{48,16},{64,32},{80,48},{96,64},{112,80},{1... | collective-permute-start | bytes 638984 | tf_op jit(solution)/shard_map/ppermute | solution.py:62
  103.9 7.6 %collective-permute-done.21.refs_1_ = f32[416,128]{1,0:T(8,128)S(1)} collective-permute-done((f32[416,128]{1,0:T(8,128)S(1)}, f32[416,128]{1,0:T(8,128)S(1)}, u32[]{:S(2)}, u32[]{:S(2)}) %collective-permute-start.21) | collective-permute-done | bytes 213024 | tf_op jit(solution)/shard_map/ppermute | solution.py:62
  113.7 4.8 %collective-permute-done.24 = f32[200,128]{1,0:T(8,128)S(1)} collective-permute-done((f32[200,128]{1,0:T(8,128)S(1)}, f32[200,128]{1,0:T(8,128)S(1)}, u32[]{:S(2)}, u32[]{:S(2)}) %collective-permute-start.24) | collective-permute-done | bytes 102432 | tf_op jit(solution)/shard_map/ppermute | solution.py:62
  119.8 2.8 collective-permute-start.26
  122.6 3.4 %collective-permute-done.27.refs_3_ = f32[400,128]{1,0:T(8,128)S(1)} collective-permute-done((f32[400,128]{1,0:T(8,128)S(1)}, f32[400,128]{1,0:T(8,128)S(1)}, u32[]{:S(2)}, u32[]{:S(2)}) %collective-permute-start.27) | collective-permute-done | bytes 204832 | tf_op jit(solution)/shard_map/ppermute | solution.py:62
  126.0 2.1 collective-permute-done.25.refs_1_
  129.8 9.8 %shard_map.93 = (f32[2,200,128]{2,1,0:T(8,128)S(1)}, f32[2,200,128]{2,1,0:T(8,128)S(1)}, f32[2,200,128]{2,1,0:T(8,128)S(1)}, f32[2,200,128]{2,1,0:T(8,128)S(1)},...) custom-call(s32[4,16]{1,0:T(4,128)S(1)} %copy.74.roster, ...), custom_call_target="tpu_custom_call" | custom-call | flops 6000000000 | bytes 6000000 | tf_op jit(solution)/shard_map/pallas_call | solution.py:365
  144.3 5.9 %shard_map.94.refs_8_ = f32[1024,400]{1,0:T(8,128)S(1)} custom-call(s32[8,128]{1,0:T(8,128)S(1)} %get-tuple-element.161.ids, f32[7424,400]{1,0:T(8,128)S(1)} %bitcast.41), custom_call_target="tpu_custom_call" | custom-call | bytes 20000000 | tf_op jit(solution)/shard_map/pallas_call | solution.py:352
  150.2 4.8 %collective-permute-done.36.plus = f32[2,200,128]{2,1,0:T(8,128)S(1)} collective-permute-done((f32[2,200,128]{2,1,0:T(8,128)S(1)}, f32[2,200,128]{2,1,0:T(8,128)S(1)}, u32[]{:S(2)}, u32[]{:S(2)}) %collective-permute-start.36) | collective-permute-done | bytes 204832 | tf_op jit(solution)/shard_map/ppermute | solution.py:84
  156.5 4.8 %collective-permute-done.39.flipped = f32[200,128]{1,0:T(8,128)S(1)} collective-permute-done((f32[200,128]{1,0:T(8,128)S(1)}, f32[200,128]{1,0:T(8,128)S(1)}, u32[]{:S(2)}, u32[]{:S(2)}) %collective-permute-start.39) | collective-permute-done | bytes 102432 | tf_op jit(solution)/shard_map/ppermute | solution.py:84
  162.3 2.3 convert_reduce_fusion.1.drawn
  166.4 3.2 %collective-permute-start.42 = (f32[416,128]{1,0:T(8,128)S(1)}, f32[416,128]{1,0:T(8,128)S(1)}, u32[]{:S(2)}, u32[]{:S(2)}) collective-permute-start(f32[416,128]{1,0:T(8,128)S(1)} %pad_maximum_fusion.2.refs_0_), channel_id=1, source_target_pairs={{0,96},{16,112},{32,0},{48,16},{64,32},{80,48},{96,64},{112,80},{1... | collective-permute-start | bytes 638984 | tf_op jit(solution)/shard_map/ppermute | solution.py:62
  169.6 4.9 %collective-permute-done.41.refs_1_ = f32[416,128]{1,0:T(8,128)S(1)} collective-permute-done((f32[416,128]{1,0:T(8,128)S(1)}, f32[416,128]{1,0:T(8,128)S(1)}, u32[]{:S(2)}, u32[]{:S(2)}) %collective-permute-start.41) | collective-permute-done | bytes 213024 | tf_op jit(solution)/shard_map/ppermute | solution.py:62
  179.1 4.8 %collective-permute-done.44 = f32[200,128]{1,0:T(8,128)S(1)} collective-permute-done((f32[200,128]{1,0:T(8,128)S(1)}, f32[200,128]{1,0:T(8,128)S(1)}, u32[]{:S(2)}, u32[]{:S(2)}) %collective-permute-start.44) | collective-permute-done | bytes 102432 | tf_op jit(solution)/shard_map/ppermute | solution.py:62
  185.6 2.8 collective-permute-start.46
  188.4 3.0 collective-permute-done.47.refs_3_
  195.2 9.8 %shard_map.97 = (f32[2,200,128]{2,1,0:T(8,128)S(1)}, f32[2,200,128]{2,1,0:T(8,128)S(1)}, f32[2,200,128]{2,1,0:T(8,128)S(1)}, f32[2,200,128]{2,1,0:T(8,128)S(1)},...) custom-call(s32[4,16]{1,0:T(4,128)S(1)} %copy.74.roster, ...), custom_call_target="tpu_custom_call" | custom-call | flops 6000000000 | bytes 6000000 | tf_op jit(solution)/shard_map/pallas_call | solution.py:365
  210.3 5.9 %shard_map.98.refs_8_ = f32[1024,400]{1,0:T(8,128)S(1)} custom-call(s32[8,128]{1,0:T(8,128)S(1)} %get-tuple-element.160.ids, f32[7424,400]{1,0:T(8,128)S(1)} %bitcast.41), custom_call_target="tpu_custom_call" | custom-call | bytes 20000000 | tf_op jit(solution)/shard_map/pallas_call | solution.py:352
  216.2 4.8 %collective-permute-done.56.plus = f32[2,200,128]{2,1,0:T(8,128)S(1)} collective-permute-done((f32[2,200,128]{2,1,0:T(8,128)S(1)}, f32[2,200,128]{2,1,0:T(8,128)S(1)}, u32[]{:S(2)}, u32[]{:S(2)}) %collective-permute-start.56) | collective-permute-done | bytes 204832 | tf_op jit(solution)/shard_map/ppermute | solution.py:84
  222.4 5.1 %collective-permute-done.59.flipped = f32[200,128]{1,0:T(8,128)S(1)} collective-permute-done((f32[200,128]{1,0:T(8,128)S(1)}, f32[200,128]{1,0:T(8,128)S(1)}, u32[]{:S(2)}, u32[]{:S(2)}) %collective-permute-start.59) | collective-permute-done | bytes 102432 | tf_op jit(solution)/shard_map/ppermute | solution.py:84
  228.5 2.3 convert_reduce_fusion.drawn
  232.6 3.2 %collective-permute-start.62 = (f32[416,128]{1,0:T(8,128)S(1)}, f32[416,128]{1,0:T(8,128)S(1)}, u32[]{:S(2)}, u32[]{:S(2)}) collective-permute-start(f32[416,128]{1,0:T(8,128)S(1)} %pad_maximum_fusion.3.refs_0_), channel_id=1, source_target_pairs={{0,96},{16,112},{32,0},{48,16},{64,32},{80,48},{96,64},{112,80},{1... | collective-permute-start | bytes 638984 | tf_op jit(solution)/shard_map/ppermute | solution.py:62
  236.4 3.4 %collective-permute-done.61.refs_1_ = f32[416,128]{1,0:T(8,128)S(1)} collective-permute-done((f32[416,128]{1,0:T(8,128)S(1)}, f32[416,128]{1,0:T(8,128)S(1)}, u32[]{:S(2)}, u32[]{:S(2)}) %collective-permute-start.61) | collective-permute-done | bytes 213024 | tf_op jit(solution)/shard_map/ppermute | solution.py:62
  245.3 5.1 %collective-permute-done.64 = f32[200,128]{1,0:T(8,128)S(1)} collective-permute-done((f32[200,128]{1,0:T(8,128)S(1)}, f32[200,128]{1,0:T(8,128)S(1)}, u32[]{:S(2)}, u32[]{:S(2)}) %collective-permute-start.64) | collective-permute-done | bytes 102432 | tf_op jit(solution)/shard_map/ppermute | solution.py:62
  251.4 2.7 collective-permute-start.66
  254.2 3.7 %collective-permute-done.67.refs_3_ = f32[400,128]{1,0:T(8,128)S(1)} collective-permute-done((f32[400,128]{1,0:T(8,128)S(1)}, f32[400,128]{1,0:T(8,128)S(1)}, u32[]{:S(2)}, u32[]{:S(2)}) %collective-permute-start.67) | collective-permute-done | bytes 204832 | tf_op jit(solution)/shard_map/ppermute | solution.py:62
  261.7 9.8 %shard_map.101 = (f32[2,200,128]{2,1,0:T(8,128)S(1)}, f32[2,200,128]{2,1,0:T(8,128)S(1)}, f32[2,200,128]{2,1,0:T(8,128)S(1)}, f32[2,200,128]{2,1,0:T(8,128)S(1)}...) custom-call(s32[4,16]{1,0:T(4,128)S(1)} %copy.74.roster, ...), custom_call_target="tpu_custom_call" | custom-call | flops 6000000000 | bytes 6000000 | tf_op jit(solution)/shard_map/pallas_call | solution.py:365
  276.2 4.9 %collective-permute-done.78.minus = f32[2,200,128]{2,1,0:T(8,128)S(1)} collective-permute-done((f32[2,200,128]{2,1,0:T(8,128)S(1)}, f32[2,200,128]{2,1,0:T(8,128)S(1)}, u32[]{:S(2)}, u32[]{:S(2)}) %collective-permute-start.78) | collective-permute-done | bytes 204832 | tf_op jit(solution)/shard_map/ppermute | solution.py:84
  281.0 5.8 %collective-permute-done.76.plus = f32[2,200,128]{2,1,0:T(8,128)S(1)} collective-permute-done((f32[2,200,128]{2,1,0:T(8,128)S(1)}, f32[2,200,128]{2,1,0:T(8,128)S(1)}, u32[]{:S(2)}, u32[]{:S(2)}) %collective-permute-start.76) | collective-permute-done | bytes 204832 | tf_op jit(solution)/shard_map/ppermute | solution.py:84
  288.3 5.1 %collective-permute-done.79.flipped = f32[200,128]{1,0:T(8,128)S(1)} collective-permute-done((f32[200,128]{1,0:T(8,128)S(1)}, f32[200,128]{1,0:T(8,128)S(1)}, u32[]{:S(2)}, u32[]{:S(2)}) %collective-permute-start.79) | collective-permute-done | bytes 102432 | tf_op jit(solution)/shard_map/ppermute | solution.py:84
  294.3 4.1 %collective-permute-done.80 = f32[208,128]{1,0:T(8,128)S(1)} collective-permute-done((f32[208,128]{1,0:T(8,128)S(1)}, f32[208,128]{1,0:T(8,128)S(1)}, u32[]{:S(2)}, u32[]{:S(2)}) %collective-permute-start.80) | collective-permute-done | bytes 106528 | tf_op jit(solution)/shard_map/ppermute | solution.py:62
  298.9 2.8 collective-permute-start.82
  301.7 3.8 %collective-permute-done.81.refs_1_ = f32[416,128]{1,0:T(8,128)S(1)} collective-permute-done((f32[416,128]{1,0:T(8,128)S(1)}, f32[416,128]{1,0:T(8,128)S(1)}, u32[]{:S(2)}, u32[]{:S(2)}) %collective-permute-start.81) | collective-permute-done | bytes 213024 | tf_op jit(solution)/shard_map/ppermute | solution.py:62
  (206 shorter events, 80.6 us)
Async XLA Ops:
  2.6 14.3 %collective-permute-start = (f32[208,128]{1,0:T(8,128)S(1)}, f32[208,128]{1,0:T(8,128)S(1)}, u32[]{:S(2)}, u32[]{:S(2)}) collective-permute-start(f32[208,128]{1,0:T(8,128)S(1)} %pad_maximum_fusion.5), channel_id=1, source_target_pairs={{0,16},{16,0},{32,48},{48,32},{64,80},{80,64},{96,112},{112,96},{1... | collective-permute-start | bytes 319496 | tf_op jit(solution)/shard_map/ppermute | solution.py:62
  5.2 31.3 %all-to-all-start = ((s32[128,1,128]{2,1,0:T(1,128)}), s32[128,1,128]{2,1,0:T(1,128)S(1)}, u32[]{:S(2)}, u32[]{:S(2)}) async-start(s32[128,1,128]{2,1,0:T(1,128)} %copy.64), calls=%async_computation | async-start | bytes 131072 | tf_op jit(solution)/shard_map/all_to_all | solution.py:395
  17.0 19.6 %collective-permute-start.1 = (f32[416,128]{1,0:T(8,128)S(1)}, f32[416,128]{1,0:T(8,128)S(1)}, u32[]{:S(2)}, u32[]{:S(2)}) collective-permute-start(f32[416,128]{1,0:T(8,128)S(1)} %pad_maximum_fusion.refs_0_), channel_id=1, source_target_pairs={{0,64},{16,80},{32,96},{48,112},{64,0},{80,16},{96,32},{112,48},{1... | collective-permute-start | bytes 638984 | tf_op jit(solution)/shard_map/ppermute | solution.py:62
  20.6 16.0 %collective-permute-start.2 = (f32[416,128]{1,0:T(8,128)S(1)}, f32[416,128]{1,0:T(8,128)S(1)}, u32[]{:S(2)}, u32[]{:S(2)}) collective-permute-start(f32[416,128]{1,0:T(8,128)S(1)} %pad_maximum_fusion.refs_0_), channel_id=1, source_target_pairs={{0,32},{16,48},{32,64},{48,80},{64,96},{80,112},{96,0},{112,16},{1... | collective-permute-start | bytes 638984 | tf_op jit(solution)/shard_map/ppermute | solution.py:62
  21.4 15.2 %collective-permute-start.3 = (f32[416,128]{1,0:T(8,128)S(1)}, f32[416,128]{1,0:T(8,128)S(1)}, u32[]{:S(2)}, u32[]{:S(2)}) collective-permute-start(f32[416,128]{1,0:T(8,128)S(1)} %pad_maximum_fusion.refs_0_), channel_id=1, source_target_pairs={{0,96},{16,112},{32,0},{48,16},{64,32},{80,48},{96,64},{112,80},{1... | collective-permute-start | bytes 638984 | tf_op jit(solution)/shard_map/ppermute | solution.py:62
  37.4 6.2 %collective-permute-start.4 = (f32[200,128]{1,0:T(8,128)S(1)}, f32[200,128]{1,0:T(8,128)S(1)}, u32[]{:S(2)}, u32[]{:S(2)}) collective-permute-start(f32[200,128]{1,0:T(8,128)S(1)} %get-tuple-element.79.x_ref), channel_id=1, source_target_pairs={{0,8},{1,9},{2,10},{3,11},{4,12},{5,13},{6,14},{7,15},{8,0},{9,1},... | collective-permute-start | bytes 307208 | tf_op jit(solution)/shard_map/ppermute | solution.py:62
  43.7 16.4 %collective-permute-start.7 = (f32[400,128]{1,0:T(8,128)S(1)}, f32[400,128]{1,0:T(8,128)S(1)}, u32[]{:S(2)}, u32[]{:S(2)}) collective-permute-start(f32[400,128]{1,0:T(8,128)S(1)} %constant_dynamic-update-slice_fusion.refs_0_), channel_id=1, source_target_pairs={{0,4},{1,5},{2,6},{3,7},{4,0},{5,1},{6,2},{7,3},{8,12},{9,13},{10,... | collective-permute-start | bytes 614408 | tf_op jit(solution)/shard_map/ppermute | solution.py:62
  46.8 13.9 %collective-permute-start.6 = (f32[400,128]{1,0:T(8,128)S(1)}, f32[400,128]{1,0:T(8,128)S(1)}, u32[]{:S(2)}, u32[]{:S(2)}) collective-permute-start(f32[400,128]{1,0:T(8,128)S(1)} %constant_dynamic-update-slice_fusion.refs_0_), channel_id=1, source_target_pairs={{0,6},{1,7},{2,0},{3,1},{4,2},{5,3},{6,4},{7,5},{8,14},{9,15},{10,... | collective-permute-start | bytes 614408 | tf_op jit(solution)/shard_map/ppermute | solution.py:62
  47.9 12.8 %collective-permute-start.5 = (f32[400,128]{1,0:T(8,128)S(1)}, f32[400,128]{1,0:T(8,128)S(1)}, u32[]{:S(2)}, u32[]{:S(2)}) collective-permute-start(f32[400,128]{1,0:T(8,128)S(1)} %constant_dynamic-update-slice_fusion.refs_0_), channel_id=1, source_target_pairs={{0,2},{1,3},{2,4},{3,5},{4,6},{5,7},{6,0},{7,1},{8,10},{9,11},{10,... | collective-permute-start | bytes 614408 | tf_op jit(solution)/shard_map/ppermute | solution.py:62
  73.1 12.3 %collective-permute-start.12 = (f32[2,200,128]{2,1,0:T(8,128)S(1)}, f32[2,200,128]{2,1,0:T(8,128)S(1)}, u32[]{:S(2)}, u32[]{:S(2)}) collective-permute-start(f32[2,200,128]{2,1,0:T(8,128)S(1)} %get-tuple-element.86), channel_id=1, source_target_pairs={{0,1},{1,0},{2,3},{3,2},{4,5},{5,4},{6,7},{7,6},{8,9},{9,8},{10,11... | collective-permute-start | bytes 614408 | tf_op jit(solution)/shard_map/ppermute | solution.py:84
  73.8 11.7 %collective-permute-start.18 = (f32[2,200,128]{2,1,0:T(8,128)S(1)}, f32[2,200,128]{2,1,0:T(8,128)S(1)}, u32[]{:S(2)}, u32[]{:S(2)}) collective-permute-start(f32[2,200,128]{2,1,0:T(8,128)S(1)} %add.197), channel_id=1, source_target_pairs={{0,6},{1,7},{2,0},{3,1},{4,2},{5,3},{6,4},{7,5},{8,14},{9,15},{10,... | collective-permute-start | bytes 614408 | tf_op jit(solution)/shard_map/ppermute | solution.py:84
  76.3 12.7 %collective-permute-start.16 = (f32[2,200,128]{2,1,0:T(8,128)S(1)}, f32[2,200,128]{2,1,0:T(8,128)S(1)}, u32[]{:S(2)}, u32[]{:S(2)}) collective-permute-start(f32[2,200,128]{2,1,0:T(8,128)S(1)} %add.196), channel_id=1, source_target_pairs={{0,2},{1,3},{2,4},{3,5},{4,6},{5,7},{6,0},{7,1},{8,10},{9,11},{10,... | collective-permute-start | bytes 614408 | tf_op jit(solution)/shard_map/ppermute | solution.py:84
  76.4 12.6 %collective-permute-start.14 = (f32[2,200,128]{2,1,0:T(8,128)S(1)}, f32[2,200,128]{2,1,0:T(8,128)S(1)}, u32[]{:S(2)}, u32[]{:S(2)}) collective-permute-start(f32[2,200,128]{2,1,0:T(8,128)S(1)} %add.195), channel_id=1, source_target_pairs={{0,4},{1,5},{2,6},{3,7},{4,0},{5,1},{6,2},{7,3},{8,12},{9,13},{10,... | collective-permute-start | bytes 614408 | tf_op jit(solution)/shard_map/ppermute | solution.py:84
  100.2 11.3 %collective-permute-start.21 = (f32[416,128]{1,0:T(8,128)S(1)}, f32[416,128]{1,0:T(8,128)S(1)}, u32[]{:S(2)}, u32[]{:S(2)}) collective-permute-start(f32[416,128]{1,0:T(8,128)S(1)} %pad_maximum_fusion.1.refs_0_), channel_id=1, source_target_pairs={{0,32},{16,48},{32,64},{48,80},{64,96},{80,112},{96,0},{112,16},{1... | collective-permute-start | bytes 638984 | tf_op jit(solution)/shard_map/ppermute | solution.py:62
  100.3 11.2 %collective-permute-start.22 = (f32[416,128]{1,0:T(8,128)S(1)}, f32[416,128]{1,0:T(8,128)S(1)}, u32[]{:S(2)}, u32[]{:S(2)}) collective-permute-start(f32[416,128]{1,0:T(8,128)S(1)} %pad_maximum_fusion.1.refs_0_), channel_id=1, source_target_pairs={{0,96},{16,112},{32,0},{48,16},{64,32},{80,48},{96,64},{112,80},{1... | collective-permute-start | bytes 638984 | tf_op jit(solution)/shard_map/ppermute | solution.py:62
  103.5 8.0 %collective-permute-start.23 = (f32[416,128]{1,0:T(8,128)S(1)}, f32[416,128]{1,0:T(8,128)S(1)}, u32[]{:S(2)}, u32[]{:S(2)}) collective-permute-start(f32[416,128]{1,0:T(8,128)S(1)} %pad_maximum_fusion.1.refs_0_), channel_id=1, source_target_pairs={{0,64},{16,80},{32,96},{48,112},{64,0},{80,16},{96,32},{112,48},{1... | collective-permute-start | bytes 638984 | tf_op jit(solution)/shard_map/ppermute | solution.py:62
  118.5 7.4 %collective-permute-start.27 = (f32[400,128]{1,0:T(8,128)S(1)}, f32[400,128]{1,0:T(8,128)S(1)}, u32[]{:S(2)}, u32[]{:S(2)}) collective-permute-start(f32[400,128]{1,0:T(8,128)S(1)} %constant_dynamic-update-slice_fusion.2.refs_0_), channel_id=1, source_target_pairs={{0,4},{1,5},{2,6},{3,7},{4,0},{5,1},{6,2},{7,3},{8,12},{9,13},{10,... | collective-permute-start | bytes 614408 | tf_op jit(solution)/shard_map/ppermute | solution.py:62
  119.4 8.7 %collective-permute-start.25 = (f32[400,128]{1,0:T(8,128)S(1)}, f32[400,128]{1,0:T(8,128)S(1)}, u32[]{:S(2)}, u32[]{:S(2)}) collective-permute-start(f32[400,128]{1,0:T(8,128)S(1)} %constant_dynamic-update-slice_fusion.2.refs_0_), channel_id=1, source_target_pairs={{0,2},{1,3},{2,4},{3,5},{4,6},{5,7},{6,0},{7,1},{8,10},{9,11},{10,... | collective-permute-start | bytes 614408 | tf_op jit(solution)/shard_map/ppermute | solution.py:62
  119.8 8.2 %collective-permute-start.26 = (f32[400,128]{1,0:T(8,128)S(1)}, f32[400,128]{1,0:T(8,128)S(1)}, u32[]{:S(2)}, u32[]{:S(2)}) collective-permute-start(f32[400,128]{1,0:T(8,128)S(1)} %constant_dynamic-update-slice_fusion.2.refs_0_), channel_id=1, source_target_pairs={{0,6},{1,7},{2,0},{3,1},{4,2},{5,3},{6,4},{7,5},{8,14},{9,15},{10,... | collective-permute-start | bytes 614408 | tf_op jit(solution)/shard_map/ppermute | solution.py:62
  140.4 9.8 %collective-permute-start.32 = (f32[2,200,128]{2,1,0:T(8,128)S(1)}, f32[2,200,128]{2,1,0:T(8,128)S(1)}, u32[]{:S(2)}, u32[]{:S(2)}) collective-permute-start(f32[2,200,128]{2,1,0:T(8,128)S(1)} %get-tuple-element.104), channel_id=1, source_target_pairs={{0,1},{1,0},{2,3},{3,2},{4,5},{5,4},{6,7},{7,6},{8,9},{9,8},{10,11... | collective-permute-start | bytes 614408 | tf_op jit(solution)/shard_map/ppermute | solution.py:84
  141.2 9.0 %collective-permute-start.38 = (f32[2,200,128]{2,1,0:T(8,128)S(1)}, f32[2,200,128]{2,1,0:T(8,128)S(1)}, u32[]{:S(2)}, u32[]{:S(2)}) collective-permute-start(f32[2,200,128]{2,1,0:T(8,128)S(1)} %add.208), channel_id=1, source_target_pairs={{0,6},{1,7},{2,0},{3,1},{4,2},{5,3},{6,4},{7,5},{8,14},{9,15},{10,... | collective-permute-start | bytes 614408 | tf_op jit(solution)/shard_map/ppermute | solution.py:84
  142.5 12.5 %collective-permute-start.36 = (f32[2,200,128]{2,1,0:T(8,128)S(1)}, f32[2,200,128]{2,1,0:T(8,128)S(1)}, u32[]{:S(2)}, u32[]{:S(2)}) collective-permute-start(f32[2,200,128]{2,1,0:T(8,128)S(1)} %add.207), channel_id=1, source_target_pairs={{0,2},{1,3},{2,4},{3,5},{4,6},{5,7},{6,0},{7,1},{8,10},{9,11},{10,... | collective-permute-start | bytes 614408 | tf_op jit(solution)/shard_map/ppermute | solution.py:84
  143.4 11.6 %collective-permute-start.34 = (f32[2,200,128]{2,1,0:T(8,128)S(1)}, f32[2,200,128]{2,1,0:T(8,128)S(1)}, u32[]{:S(2)}, u32[]{:S(2)}) collective-permute-start(f32[2,200,128]{2,1,0:T(8,128)S(1)} %add.206), channel_id=1, source_target_pairs={{0,4},{1,5},{2,6},{3,7},{4,0},{5,1},{6,2},{7,3},{8,12},{9,13},{10,... | collective-permute-start | bytes 614408 | tf_op jit(solution)/shard_map/ppermute | solution.py:84
  166.3 8.2 %collective-permute-start.41 = (f32[416,128]{1,0:T(8,128)S(1)}, f32[416,128]{1,0:T(8,128)S(1)}, u32[]{:S(2)}, u32[]{:S(2)}) collective-permute-start(f32[416,128]{1,0:T(8,128)S(1)} %pad_maximum_fusion.2.refs_0_), channel_id=1, source_target_pairs={{0,32},{16,48},{32,64},{48,80},{64,96},{80,112},{96,0},{112,16},{1... | collective-permute-start | bytes 638984 | tf_op jit(solution)/shard_map/ppermute | solution.py:62
  166.4 8.9 %collective-permute-start.42 = (f32[416,128]{1,0:T(8,128)S(1)}, f32[416,128]{1,0:T(8,128)S(1)}, u32[]{:S(2)}, u32[]{:S(2)}) collective-permute-start(f32[416,128]{1,0:T(8,128)S(1)} %pad_maximum_fusion.2.refs_0_), channel_id=1, source_target_pairs={{0,96},{16,112},{32,0},{48,16},{64,32},{80,48},{96,64},{112,80},{1... | collective-permute-start | bytes 638984 | tf_op jit(solution)/shard_map/ppermute | solution.py:62
  169.6 7.3 %collective-permute-start.43 = (f32[416,128]{1,0:T(8,128)S(1)}, f32[416,128]{1,0:T(8,128)S(1)}, u32[]{:S(2)}, u32[]{:S(2)}) collective-permute-start(f32[416,128]{1,0:T(8,128)S(1)} %pad_maximum_fusion.2.refs_0_), channel_id=1, source_target_pairs={{0,64},{16,80},{32,96},{48,112},{64,0},{80,16},{96,32},{112,48},{1... | collective-permute-start | bytes 638984 | tf_op jit(solution)/shard_map/ppermute | solution.py:62
  183.9 7.4 %collective-permute-start.47 = (f32[400,128]{1,0:T(8,128)S(1)}, f32[400,128]{1,0:T(8,128)S(1)}, u32[]{:S(2)}, u32[]{:S(2)}) collective-permute-start(f32[400,128]{1,0:T(8,128)S(1)} %constant_dynamic-update-slice_fusion.4.refs_0_), channel_id=1, source_target_pairs={{0,4},{1,5},{2,6},{3,7},{4,0},{5,1},{6,2},{7,3},{8,12},{9,13},{10,... | collective-permute-start | bytes 614408 | tf_op jit(solution)/shard_map/ppermute | solution.py:62
  185.2 8.3 %collective-permute-start.45 = (f32[400,128]{1,0:T(8,128)S(1)}, f32[400,128]{1,0:T(8,128)S(1)}, u32[]{:S(2)}, u32[]{:S(2)}) collective-permute-start(f32[400,128]{1,0:T(8,128)S(1)} %constant_dynamic-update-slice_fusion.4.refs_0_), channel_id=1, source_target_pairs={{0,2},{1,3},{2,4},{3,5},{4,6},{5,7},{6,0},{7,1},{8,10},{9,11},{10,... | collective-permute-start | bytes 614408 | tf_op jit(solution)/shard_map/ppermute | solution.py:62
  185.6 7.8 %collective-permute-start.46 = (f32[400,128]{1,0:T(8,128)S(1)}, f32[400,128]{1,0:T(8,128)S(1)}, u32[]{:S(2)}, u32[]{:S(2)}) collective-permute-start(f32[400,128]{1,0:T(8,128)S(1)} %constant_dynamic-update-slice_fusion.4.refs_0_), channel_id=1, source_target_pairs={{0,6},{1,7},{2,0},{3,1},{4,2},{5,3},{6,4},{7,5},{8,14},{9,15},{10,... | collective-permute-start | bytes 614408 | tf_op jit(solution)/shard_map/ppermute | solution.py:62
  206.0 10.2 %collective-permute-start.52 = (f32[2,200,128]{2,1,0:T(8,128)S(1)}, f32[2,200,128]{2,1,0:T(8,128)S(1)}, u32[]{:S(2)}, u32[]{:S(2)}) collective-permute-start(f32[2,200,128]{2,1,0:T(8,128)S(1)} %get-tuple-element.122), channel_id=1, source_target_pairs={{0,1},{1,0},{2,3},{3,2},{4,5},{5,4},{6,7},{7,6},{8,9},{9,8},{10,11... | collective-permute-start | bytes 614408 | tf_op jit(solution)/shard_map/ppermute | solution.py:84
  206.6 9.6 %collective-permute-start.58 = (f32[2,200,128]{2,1,0:T(8,128)S(1)}, f32[2,200,128]{2,1,0:T(8,128)S(1)}, u32[]{:S(2)}, u32[]{:S(2)}) collective-permute-start(f32[2,200,128]{2,1,0:T(8,128)S(1)} %add.219), channel_id=1, source_target_pairs={{0,6},{1,7},{2,0},{3,1},{4,2},{5,3},{6,4},{7,5},{8,14},{9,15},{10,... | collective-permute-start | bytes 614408 | tf_op jit(solution)/shard_map/ppermute | solution.py:84
  208.5 12.5 %collective-permute-start.56 = (f32[2,200,128]{2,1,0:T(8,128)S(1)}, f32[2,200,128]{2,1,0:T(8,128)S(1)}, u32[]{:S(2)}, u32[]{:S(2)}) collective-permute-start(f32[2,200,128]{2,1,0:T(8,128)S(1)} %add.218), channel_id=1, source_target_pairs={{0,2},{1,3},{2,4},{3,5},{4,6},{5,7},{6,0},{7,1},{8,10},{9,11},{10,... | collective-permute-start | bytes 614408 | tf_op jit(solution)/shard_map/ppermute | solution.py:84
  208.8 12.1 %collective-permute-start.54 = (f32[2,200,128]{2,1,0:T(8,128)S(1)}, f32[2,200,128]{2,1,0:T(8,128)S(1)}, u32[]{:S(2)}, u32[]{:S(2)}) collective-permute-start(f32[2,200,128]{2,1,0:T(8,128)S(1)} %add.217), channel_id=1, source_target_pairs={{0,4},{1,5},{2,6},{3,7},{4,0},{5,1},{6,2},{7,3},{8,12},{9,13},{10,... | collective-permute-start | bytes 614408 | tf_op jit(solution)/shard_map/ppermute | solution.py:84
  221.0 6.5 %collective-permute-start.59 = (f32[200,128]{1,0:T(8,128)S(1)}, f32[200,128]{1,0:T(8,128)S(1)}, u32[]{:S(2)}, u32[]{:S(2)}) collective-permute-start(f32[200,128]{1,0:T(8,128)S(1)} %fusion.4), channel_id=1, source_target_pairs={{0,8},{1,9},{2,10},{3,11},{4,12},{5,13},{6,14},{7,15},{8,0},{9,1},... | collective-permute-start | bytes 307208 | tf_op jit(solution)/shard_map/ppermute | solution.py:84
  232.5 7.2 %collective-permute-start.61 = (f32[416,128]{1,0:T(8,128)S(1)}, f32[416,128]{1,0:T(8,128)S(1)}, u32[]{:S(2)}, u32[]{:S(2)}) collective-permute-start(f32[416,128]{1,0:T(8,128)S(1)} %pad_maximum_fusion.3.refs_0_), channel_id=1, source_target_pairs={{0,32},{16,48},{32,64},{48,80},{64,96},{80,112},{96,0},{112,16},{1... | collective-permute-start | bytes 638984 | tf_op jit(solution)/shard_map/ppermute | solution.py:62
  232.6 8.9 %collective-permute-start.62 = (f32[416,128]{1,0:T(8,128)S(1)}, f32[416,128]{1,0:T(8,128)S(1)}, u32[]{:S(2)}, u32[]{:S(2)}) collective-permute-start(f32[416,128]{1,0:T(8,128)S(1)} %pad_maximum_fusion.3.refs_0_), channel_id=1, source_target_pairs={{0,96},{16,112},{32,0},{48,16},{64,32},{80,48},{96,64},{112,80},{1... | collective-permute-start | bytes 638984 | tf_op jit(solution)/shard_map/ppermute | solution.py:62
  235.8 7.5 %collective-permute-start.63 = (f32[416,128]{1,0:T(8,128)S(1)}, f32[416,128]{1,0:T(8,128)S(1)}, u32[]{:S(2)}, u32[]{:S(2)}) collective-permute-start(f32[416,128]{1,0:T(8,128)S(1)} %pad_maximum_fusion.3.refs_0_), channel_id=1, source_target_pairs={{0,64},{16,80},{32,96},{48,112},{64,0},{80,16},{96,32},{112,48},{1... | collective-permute-start | bytes 638984 | tf_op jit(solution)/shard_map/ppermute | solution.py:62
  250.4 7.4 %collective-permute-start.67 = (f32[400,128]{1,0:T(8,128)S(1)}, f32[400,128]{1,0:T(8,128)S(1)}, u32[]{:S(2)}, u32[]{:S(2)}) collective-permute-start(f32[400,128]{1,0:T(8,128)S(1)} %constant_dynamic-update-slice_fusion.6.refs_0_), channel_id=1, source_target_pairs={{0,4},{1,5},{2,6},{3,7},{4,0},{5,1},{6,2},{7,3},{8,12},{9,13},{10,... | collective-permute-start | bytes 614408 | tf_op jit(solution)/shard_map/ppermute | solution.py:62
  250.9 9.0 %collective-permute-start.65 = (f32[400,128]{1,0:T(8,128)S(1)}, f32[400,128]{1,0:T(8,128)S(1)}, u32[]{:S(2)}, u32[]{:S(2)}) collective-permute-start(f32[400,128]{1,0:T(8,128)S(1)} %constant_dynamic-update-slice_fusion.6.refs_0_), channel_id=1, source_target_pairs={{0,2},{1,3},{2,4},{3,5},{4,6},{5,7},{6,0},{7,1},{8,10},{9,11},{10,... | collective-permute-start | bytes 614408 | tf_op jit(solution)/shard_map/ppermute | solution.py:62
  251.4 8.5 %collective-permute-start.66 = (f32[400,128]{1,0:T(8,128)S(1)}, f32[400,128]{1,0:T(8,128)S(1)}, u32[]{:S(2)}, u32[]{:S(2)}) collective-permute-start(f32[400,128]{1,0:T(8,128)S(1)} %constant_dynamic-update-slice_fusion.6.refs_0_), channel_id=1, source_target_pairs={{0,6},{1,7},{2,0},{3,1},{4,2},{5,3},{6,4},{7,5},{8,14},{9,15},{10,... | collective-permute-start | bytes 614408 | tf_op jit(solution)/shard_map/ppermute | solution.py:62
  254.2 6.3 %collective-permute-start.68 = (f32[400,128]{1,0:T(8,128)S(1)}, f32[400,128]{1,0:T(8,128)S(1)}, u32[]{:S(2)}, u32[]{:S(2)}) collective-permute-start(f32[400,128]{1,0:T(8,128)S(1)} %constant_dynamic-update-slice_fusion.6.refs_0_), channel_id=1, source_target_pairs={{0,1},{1,0},{2,3},{3,2},{4,5},{5,4},{6,7},{7,6},{8,9},{9,8},{10,11... | collective-permute-start | bytes 614408 | tf_op jit(solution)/shard_map/ppermute | solution.py:77
  273.1 8.0 %collective-permute-start.78 = (f32[2,200,128]{2,1,0:T(8,128)S(1)}, f32[2,200,128]{2,1,0:T(8,128)S(1)}, u32[]{:S(2)}, u32[]{:S(2)}) collective-permute-start(f32[2,200,128]{2,1,0:T(8,128)S(1)} %add.230), channel_id=1, source_target_pairs={{0,6},{1,7},{2,0},{3,1},{4,2},{5,3},{6,4},{7,5},{8,14},{9,15},{10,... | collective-permute-start | bytes 614408 | tf_op jit(solution)/shard_map/ppermute | solution.py:84
  274.1 12.8 %collective-permute-start.76 = (f32[2,200,128]{2,1,0:T(8,128)S(1)}, f32[2,200,128]{2,1,0:T(8,128)S(1)}, u32[]{:S(2)}, u32[]{:S(2)}) collective-permute-start(f32[2,200,128]{2,1,0:T(8,128)S(1)} %add.229), channel_id=1, source_target_pairs={{0,2},{1,3},{2,4},{3,5},{4,6},{5,7},{6,0},{7,1},{8,10},{9,11},{10,... | collective-permute-start | bytes 614408 | tf_op jit(solution)/shard_map/ppermute | solution.py:84
  275.5 11.3 %collective-permute-start.74 = (f32[2,200,128]{2,1,0:T(8,128)S(1)}, f32[2,200,128]{2,1,0:T(8,128)S(1)}, u32[]{:S(2)}, u32[]{:S(2)}) collective-permute-start(f32[2,200,128]{2,1,0:T(8,128)S(1)} %add.228), channel_id=1, source_target_pairs={{0,4},{1,5},{2,6},{3,7},{4,0},{5,1},{6,2},{7,3},{8,12},{9,13},{10,... | collective-permute-start | bytes 614408 | tf_op jit(solution)/shard_map/ppermute | solution.py:84
  286.9 6.5 %collective-permute-start.79 = (f32[200,128]{1,0:T(8,128)S(1)}, f32[200,128]{1,0:T(8,128)S(1)}, u32[]{:S(2)}, u32[]{:S(2)}) collective-permute-start(f32[200,128]{1,0:T(8,128)S(1)} %fusion.1), channel_id=1, source_target_pairs={{0,8},{1,9},{2,10},{3,11},{4,12},{5,13},{6,14},{7,15},{8,0},{9,1},... | collective-permute-start | bytes 307208 | tf_op jit(solution)/shard_map/ppermute | solution.py:84
  298.4 7.1 %collective-permute-start.81 = (f32[416,128]{1,0:T(8,128)S(1)}, f32[416,128]{1,0:T(8,128)S(1)}, u32[]{:S(2)}, u32[]{:S(2)}) collective-permute-start(f32[416,128]{1,0:T(8,128)S(1)} %pad_maximum_fusion.4.refs_0_), channel_id=1, source_target_pairs={{0,32},{16,48},{32,64},{48,80},{64,96},{80,112},{96,0},{112,16},{1... | collective-permute-start | bytes 638984 | tf_op jit(solution)/shard_map/ppermute | solution.py:62
  298.9 8.4 %collective-permute-start.82 = (f32[416,128]{1,0:T(8,128)S(1)}, f32[416,128]{1,0:T(8,128)S(1)}, u32[]{:S(2)}, u32[]{:S(2)}) collective-permute-start(f32[416,128]{1,0:T(8,128)S(1)} %pad_maximum_fusion.4.refs_0_), channel_id=1, source_target_pairs={{0,96},{16,112},{32,0},{48,16},{64,32},{80,48},{96,64},{112,80},{1... | collective-permute-start | bytes 638984 | tf_op jit(solution)/shard_map/ppermute | solution.py:62
  301.7 7.3 %collective-permute-start.83 = (f32[416,128]{1,0:T(8,128)S(1)}, f32[416,128]{1,0:T(8,128)S(1)}, u32[]{:S(2)}, u32[]{:S(2)}) collective-permute-start(f32[416,128]{1,0:T(8,128)S(1)} %pad_maximum_fusion.4.refs_0_), channel_id=1, source_target_pairs={{0,64},{16,80},{32,96},{48,112},{64,0},{80,16},{96,32},{112,48},{1... | collective-permute-start | bytes 638984 | tf_op jit(solution)/shard_map/ppermute | solution.py:62
  (43 other events, 246.0 us)
